TPU v7x, 256 devices: a whole 4x4x8 slice. The times are simulated.
256 devices in a mesh: ctx: 64 (over z, y, x_lo), fsdp: 4 (over x_hi, core).
Axes of the slice: x: 4 (x_hi: 2, x_lo: 2; x = x_hi * 2 + x_lo), y: 4, z: 8, core: 2. Of those that a mesh axis runs over, the one named last changes fastest.
Arguments:
- video_query: bfloat16 [4, 32768, 1024], P('fsdp', 'ctx'), may hold values from -256 to 256
- audio_key: bfloat16 [4, 512, 1024], P('fsdp', 'ctx'), may hold values from -9 to 9
- audio_value: bfloat16 [4, 512, 1024], P('fsdp', 'ctx'), may hold values from -6 to 6
- out_weight: bfloat16 [1024, 4096], P(None, 'fsdp'), may hold values from -0.1875 to 0.1875
- grad_out: bfloat16 [4, 32768, 4096], P('fsdp', 'ctx'), may hold values from -6 to 6
- query_time: int32 [32768], P('ctx'), may hold values from 0 to 511, as said below
- window: int32 [2, 32768], P(None, 'ctx'), may hold values from 0 to 512, as said below
Outputs:
- output: bfloat16 [4, 32768, 4096], P('fsdp', 'ctx')
- query_grad: bfloat16 [4, 32768, 1024], P('fsdp', 'ctx')
- key_grad: float32 [4, 512, 1024], P('fsdp', 'ctx')
- value_grad: float32 [4, 512, 1024], P('fsdp', 'ctx')
- weight_grad: float32 [1024, 4096], P('ctx', 'fsdp')
Inputs may be any that keep to these rules, and one draw needn't show every extreme that they name: query_time of video token i lies in [window[0, i], window[1, i]). For video token i, with d = i // 512: max(0, (d - 1) * 8) <= window[0, i] < window[1, i] <= min(512, (d + 2) * 8); both bounds are reached by some token of every d.
All inputs are finite; a program needn't handle non-finite values.
Results may differ from a plain program's by a relative error of at most 0.027.
The roundings to bfloat16 on the way count: a program that leaves them out, or rounds other values in their place, can miss the bound.
Values may be sent and summed in bfloat16 or wider, within the bound.
A program may use at most 128 MiB of HBM per device.

v0:
```python
import math

import jax
import jax.numpy as jnp
from jax import lax
from jax.sharding import PartitionSpec as P

DH = 64


def padded(block, sides, width):
    for axis, dim in sides:
        count = lax.axis_size(axis)
        forward = [(i, i + 1) for i in range(count - 1)]
        backward = [(target, source) for source, target in forward]
        low = lax.ppermute(
            lax.slice_in_dim(block, block.shape[dim] - width, None, axis=dim), axis, forward
        )
        high = lax.ppermute(lax.slice_in_dim(block, 0, width, axis=dim), axis, backward)
        block = jnp.concatenate([low, block, high], axis=dim)
    return block


def shifted(block, axis, distance):
    devices = range(lax.axis_size(axis))
    route = [(i - distance, i) for i in devices if i - distance in devices]
    return lax.ppermute(block, axis, route)


def rotate(values, positions, sign):
    heads = values.shape[-1] // DH
    half = DH // 2
    shaped = values.astype(jnp.float32).reshape(values.shape[:-1] + (heads, DH))
    freqs = 10000.0 ** (-jnp.arange(half, dtype=jnp.float32) / half)
    angles = sign * positions.astype(jnp.float32)[:, None] * freqs[None, :]
    cosine = jnp.cos(angles)[:, None, :]
    sine = jnp.sin(angles)[:, None, :]
    first = shaped[..., :half]
    second = shaped[..., half:]
    turned = jnp.concatenate(
        [first * cosine - second * sine, first * sine + second * cosine], axis=-1
    )
    return turned.reshape(values.shape)


def local(video_query, audio_key, audio_value, out_weight, grad_out, query_time, window):
    own_span = audio_key.shape[1]
    rows = video_query.shape[1]
    width = video_query.shape[2]
    heads = width // DH
    near_span = 3 * own_span
    scale = 1.0 / math.sqrt(DH)
    shard = lax.axis_index("ctx")
    key_index = shard * own_span + jnp.arange(own_span, dtype=jnp.int32)
    key_rot = rotate(audio_key[0], key_index, 1.0).astype(jnp.bfloat16)
    query_rot = rotate(video_query[0], query_time, 1.0).astype(jnp.bfloat16)
    paired = jnp.stack([key_rot, audio_value[0]])
    reached = padded(paired, (("ctx", 1),), own_span)
    key_heads = reached[0].reshape(near_span, heads, DH)
    value_heads = reached[1].reshape(near_span, heads, DH)
    near_index = shard * own_span - own_span + jnp.arange(near_span, dtype=jnp.int32)
    allowed = (near_index[:, None] >= window[0][None, :]) & (
        near_index[:, None] < window[1][None, :]
    )
    query_heads = query_rot.reshape(rows, heads, DH)
    scores = scale * jnp.einsum(
        "qhd,khd->hkq", query_heads, key_heads, preferred_element_type=jnp.float32
    )
    masked = jnp.where(allowed, scores, -1e30)
    highest = jnp.max(masked, axis=1, keepdims=True)
    expo = jnp.where(allowed, jnp.exp(masked - highest), 0.0)
    probs = expo / jnp.sum(expo, axis=1, keepdims=True)
    probs_low = probs.astype(jnp.bfloat16)
    attended = jnp.einsum(
        "hkq,khd->qhd", probs_low, value_heads, preferred_element_type=jnp.float32
    )
    attended = attended.astype(jnp.bfloat16).reshape(rows, width)
    local_grad = grad_out[0]
    contract_last = (((1,), (1,)), ((), ()))
    output = jnp.dot(
        attended,
        lax.all_gather(out_weight, "fsdp", axis=1, tiled=True),
        preferred_element_type=jnp.float32,
    ).astype(jnp.bfloat16)
    att_grad = lax.dot_general(
        local_grad,
        lax.all_gather(out_weight, "fsdp", axis=1, tiled=True),
        contract_last,
        preferred_element_type=jnp.float32,
    )
    grad_heads = att_grad.astype(jnp.bfloat16).reshape(rows, heads, DH)
    value_part = jnp.einsum(
        "hkq,qhd->khd", probs_low, grad_heads, preferred_element_type=jnp.float32
    )
    prob_grad = jnp.einsum(
        "qhd,khd->hkq", grad_heads, value_heads, preferred_element_type=jnp.float32
    )
    row_dot = jnp.sum(probs * prob_grad, axis=1, keepdims=True)
    score_grad = (probs * (prob_grad - row_dot)).astype(jnp.bfloat16)
    query_part = scale * jnp.einsum(
        "hkq,khd->qhd", score_grad, key_heads, preferred_element_type=jnp.float32
    )
    query_grad = rotate(query_part.reshape(rows, width), query_time, -1.0).astype(jnp.bfloat16)
    key_part = scale * jnp.einsum(
        "hkq,qhd->khd", score_grad, query_heads, preferred_element_type=jnp.float32
    )
    partial_value = jnp.stack(
        [key_part.reshape(near_span, width), value_part.reshape(near_span, width)]
    )
    lower_part = partial_value[:, :own_span]
    upper_part = partial_value[:, 2 * own_span :]
    from_before = shifted(upper_part, "ctx", 1)
    from_after = shifted(lower_part, "ctx", -1)
    summed = partial_value[:, own_span : 2 * own_span] + from_before + from_after
    key_grad = rotate(summed[0], key_index, -1.0)
    value_grad = summed[1]
    factor = 1.0 / math.sqrt(rows * lax.axis_size("ctx") * lax.axis_size("fsdp"))
    contract_first = (((0,), (0,)), ((), ()))
    row_terms = lax.psum_scatter(
        factor
        * lax.dot_general(attended, local_grad, contract_first, preferred_element_type=jnp.float32),
        "ctx",
        scatter_dimension=0,
        tiled=True,
    )
    weight_grad = lax.psum_scatter(row_terms, "fsdp", scatter_dimension=1, tiled=True)
    return (output[None], query_grad[None], key_grad[None], value_grad[None], weight_grad)


def solution(mesh):
    in_specs = (
        P("fsdp", "ctx", None),
        P("fsdp", "ctx", None),
        P("fsdp", "ctx", None),
        P(None, "fsdp"),
        P("fsdp", "ctx", None),
        P("ctx"),
        P(None, "ctx"),
    )
    out_specs = (
        P("fsdp", "ctx", None),
        P("fsdp", "ctx", None),
        P("fsdp", "ctx", None),
        P("fsdp", "ctx", None),
        P("ctx", "fsdp"),
    )
    return jax.shard_map(local, mesh=mesh, in_specs=in_specs, out_specs=out_specs, check_vma=False)
```

profile of v0, /device:TPU:4, one launch (start us, length us, event | category | flops | bytes accessed | tf_op | source)
XLA Modules:
  0.0 472.5 jit_solution(9358483982595467601)
XLA Ops:
  8.1 0.7 all-gather.2.cloned.1.call-update
  8.8 0.8 reshape.259
  10.1 0.7 constant_dynamic-update-slice_fusion
  10.8 3.1 collective-permute-start
  13.9 1.3 collective-permute-start.1
  15.2 0.7 convert_element_type.77
  15.9 1.5 copy.16
  17.4 0.5 multiply_cosine_fusion
  18.4 1.3 collective-permute-done.1
  20.0 0.5 fusion.36
  20.5 0.5 convolution_convert_fusion.1
  21.0 12.5 %convolution_multiply_fusion = f32[1024,4096]{1,0:T(8,128)} fusion(bf16[512,1024]{0,1:T(8,128)(2,1)S(1)} %bitcast.37, bf16[1,512,4096]{2,1,0:T(8,128)(2,1)} %param.11), kind=kOutput, calls=%fused_computation.1 | convolution fusion | flops 4299161600 | bytes 22020096 | tf_op jit(solution)/shard_map/dot_general | solution.py:121
  33.5 45.9 %all-gather.2.cloned.1.call-done = bf16[1024,4096]{1,0:T(8,128)(2,1)} async-done(((bf16[1024,1024]{1,0:T(8,128)(2,1)}), bf16[1024,4096]{1,0:T(8,128)(2,1)}) %all-gather.2.cloned.1.call-update) | async-done | bytes 8388624 | tf_op jit(solution)/shard_map/all_gather | solution.py:82
  79.4 9.2 %fusion.5 = bf16[512,1024]{1,0:T(8,128)(2,1)S(1)} fusion(bf16[1024,4096]{1,0:T(8,128)(2,1)} %all-gather.2.cloned.1.call-done, bf16[1,512,4096]{2,1,0:T(8,128)(2,1)} %param.11), kind=kOutput, calls=%fused_computation.8 | convolution fusion | flops 4295491584 | bytes 13631488 | tf_op jit(solution)/shard_map/dot_general | solution.py:85
  88.7 0.5 copy.19
  89.8 0.5 copy-done.1
  91.6 1.3 collective-permute-start.2
  92.9 1.5 collective-permute-start.3
  95.2 10.4 %fusion.1 = bf16[1,512,4096]{2,1,0:T(8,128)(2,1)} fusion(bf16[512,1024]{0,1:T(8,128)(2,1)} %bitcast.38, bf16[1024,4096]{1,0:T(8,128)(2,1)} %all-gather.2.cloned.1.call-done), kind=kOutput, calls=%fused_computation.3 | convolution fusion | flops 4297064448 | bytes 13631488 | tf_op jit(solution)/shard_map/dot_general | solution.py:80
  105.7 1.3 copy.24
  107.0 328.1 %reduce-scatter.3.cloned.1.call-done = f32[16,4096]{1,0:T(8,128)} async-done(((f32[1024,4096]{1,0:T(8,128)}), f32[16,4096]{1,0:T(8,128)}) %reduce-scatter.3.cloned.1.call-update) | async-done | bytes 262160 | tf_op jit(solution)/shard_map/reduce_scatter | solution.py:119
  435.1 0.6 fusion.34
  436.0 0.7 broadcast_in_dim_reshape.3
  436.7 28.4 %reduce-scatter.5.cloned.1.call-done = f32[16,1024]{1,0:T(8,128)} async-done(((f32[16,4096]{1,0:T(8,128)}), f32[16,1024]{1,0:T(8,128)}) %reduce-scatter.5.cloned.1.call-update) | async-done | bytes 65552 | tf_op jit(solution)/shard_map/reduce_scatter | solution.py:126
  (56 shorter events, 4.3 us)
Async XLA Ops:
  8.0 9.4 %copy-start.4 = (s32[512]{0:T(512)S(1)}, s32[512]{0:T(512)}, u32[]{:S(2)}) copy-start(s32[512]{0:T(512)} %param.12) | copy-start | bytes 6148
  8.0 9.4 %copy-start.5 = (s32[2,512]{1,0:T(2,128)S(1)}, s32[2,512]{1,0:T(2,128)}, u32[]{:S(2)}) copy-start(s32[2,512]{1,0:T(2,128)} %param.13) | copy-start | bytes 12292
  8.0 71.4 %all-gather.2.cloned.1.call-start = ((), (), s32[]{:S(2)}) async-start(), calls=%async_computation.2 | async-start | bytes 10485760 | tf_op jit(solution)/shard_map/all_gather | solution.py:82
  8.8 426.3 %reduce-scatter.3.cloned.1.call-start = ((), (), s32[]{:S(2)}) async-start(), calls=%async_computation.3 | async-start | bytes 17039360 | tf_op jit(solution)/shard_map/reduce_scatter | solution.py:119
  10.8 7.6 %collective-permute-start = (bf16[2,8,1024]{2,1,0:T(8,128)(2,1)S(1)}, bf16[2,8,1024]{2,1,0:T(8,128)(2,1)S(1)}, u32[]{:S(2)}, u32[]{:S(2)}) collective-permute-start(bf16[2,8,1024]{2,1,0:T(8,128)(2,1)S(1)} %constant_dynamic-update-slice_fusion), channel_id=1, source_target_pairs={{0,4},{4,8},{8,12},{12,16},{16,20},{20,24},{24,28},{28,32},{32,36}... | collective-permute-start | bytes 98312 | tf_op jit(solution)/shard_map/ppermute | solution.py:16
  13.9 5.8 %collective-permute-start.1 = (bf16[2,8,1024]{2,1,0:T(8,128)(2,1)S(1)}, bf16[2,8,1024]{2,1,0:T(8,128)(2,1)S(1)}, u32[]{:S(2)}, u32[]{:S(2)}) collective-permute-start(bf16[2,8,1024]{2,1,0:T(8,128)(2,1)S(1)} %constant_dynamic-update-slice_fusion), channel_id=1, source_target_pairs={{4,0},{8,4},{12,8},{16,12},{20,16},{24,20},{28,24},{32,28},{36,32}... | collective-permute-start | bytes 98312 | tf_op jit(solution)/shard_map/ppermute | solution.py:19
  18.3 15.1 %copy-start = (bf16[512,16,32]{0,2,1:T(8,128)(2,1)}, bf16[512,16,32]{0,2,1:T(8,128)(2,1)S(1)}, u32[]{:S(2)}) copy-start(bf16[512,16,32]{0,2,1:T(8,128)(2,1)S(1)} %get-tuple-element.17) | copy-start | bytes 1572868
  18.3 15.1 %copy-start.2 = (bf16[512,16,32]{0,2,1:T(8,128)(2,1)}, bf16[512,16,32]{0,2,1:T(8,128)(2,1)S(1)}, u32[]{:S(2)}) copy-start(bf16[512,16,32]{0,2,1:T(8,128)(2,1)S(1)} %get-tuple-element.18) | copy-start | bytes 1572868
  21.0 12.5 %copy-start.6 = (bf16[16,64,512]{2,1,0:T(8,128)(2,1)}, bf16[16,64,512]{2,1,0:T(8,128)(2,1)S(1)}, u32[]{:S(2)}) copy-start(bf16[16,64,512]{2,1,0:T(8,128)(2,1)S(1)} %convolution_convert_fusion.1) | copy-start | bytes 3145732
  33.5 431.6 %reduce-scatter.5.cloned.1.call-start = ((), (), s32[]{:S(2)}) async-start(), calls=%async_computation.4 | async-start | bytes 327680 | tf_op jit(solution)/shard_map/reduce_scatter | solution.py:126
  89.2 1.0 copy-start.1
  89.2 1.2 copy-start.3
  91.6 15.4 %collective-permute-start.2 = (f32[2,8,1024]{2,1,0:T(8,128)S(1)}, f32[2,8,1024]{2,1,0:T(8,128)S(1)}, u32[]{:S(2)}, u32[]{:S(2)}) collective-permute-start(f32[2,8,1024]{2,1,0:T(8,128)S(1)} %get-tuple-element.19), channel_id=1, source_target_pairs={{0,4},{4,8},{8,12},{12,16},{16,20},{20,24},{24,28},{28,32},{32,36}... | collective-permute-start | bytes 196616 | tf_op jit(solution)/shard_map/ppermute | solution.py:27
  92.9 14.1 %collective-permute-start.3 = (f32[2,8,1024]{2,1,0:T(8,128)S(1)}, f32[2,8,1024]{2,1,0:T(8,128)S(1)}, u32[]{:S(2)}, u32[]{:S(2)}) collective-permute-start(f32[2,8,1024]{2,1,0:T(8,128)S(1)} %get-tuple-element.20), channel_id=1, source_target_pairs={{4,0},{8,4},{12,8},{16,12},{20,16},{24,20},{28,24},{32,28},{36,32}... | collective-permute-start | bytes 196616 | tf_op jit(solution)/shard_map/ppermute | solution.py:27
Sparse Core Ops, SparseCore 0:
  10.7 68.7 all-gather.1
  435.2 29.8 reduce-scatter.4
Sparse Core Ops, SparseCore 1:
  33.5 401.5 reduce-scatter.2
where the time goes:
time: 476 us; the launch traced here: 473 us
  waiting for transfers between devices  404 us (85%)
  matrix products  34.5 us (7%)
  between operations  15.8 us (3%)
  local copies, waits for them, and re-layouts  7.69 us (2%)
  starting transfers between devices  7.27 us (2%)
    reduce_scatter x1, waiting for transfers between devices, local(): lax.psum_scatter(factor * lax.dot_general(attended, local_grad, contract_...  328 us
    all_gather x1, waiting for transfers between devices, local(): lax.all_gather(out_weight, 'fsdp', axis=1, tiled=True)  45.9 us
    reduce_scatter x1, waiting for transfers between devices, local(): lax.psum_scatter(row_terms, 'fsdp', scatter_dimension=1, tiled=True)  28.4 us
    dot_general x1, matrix products, local(): lax.dot_general(attended, local_grad, contract_first, preferred_element_t...  12.5 us
    dot_general x1, matrix products, local(): jnp.dot(attended, lax.all_gather(out_weight, 'fsdp', axis=1, tiled=True),...  10.4 us
  transfers between devices with their start and end apart: 7, of which 4 were waited for; matrix products, arithmetic and copies ran while one was open for 9% of the time, Pallas kernels for 0%

commit v1 on v0

v1 whole, which is shorter than its diff:
```python
import math

import jax
import jax.numpy as jnp
import numpy as np
from jax import lax
from jax.experimental import pallas as pl
from jax.experimental.pallas import tpu as pltpu
from jax.sharding import PartitionSpec as P

DH = 64
HALF = DH // 2
TOK = 512
WIDTH = 1024
SPAN = 8
NEAR = 3 * SPAN
GROUPS = 4
GW = WIDTH // GROUPS
GH = GW // DH
SCALE = 1.0 / math.sqrt(DH)
MESH = pl.DeviceIdType.MESH
BF = jnp.bfloat16
F32 = jnp.float32

NN = (((1,), (0,)), ((), ()))
NT = (((1,), (1,)), ((), ()))
TN = (((0,), (0,)), ((), ()))


def dot(a, b, dims):
    return lax.dot_general(a, b, dims, preferred_element_type=F32)


def flip(value, mask, bits):
    out = 0
    for bit in range(bits):
        digit = (value // (1 << bit)) % 2
        if (mask >> bit) & 1:
            digit = 1 - digit
        out = out + digit * (1 << bit)
    return out


def kernel(
    factor,
    query_hbm,
    key_ref,
    value_ref,
    weight_hbm,
    grad_hbm,
    cos_ref,
    sin_ref,
    window_ref,
    out_hbm,
    qgrad_hbm,
    kgrad_ref,
    vgrad_ref,
    wgrad_ref,
    q_raw,
    q_rot,
    near_kv,
    w_all,
    g_own,
    g_pair,
    probs_s,
    att,
    att_t,
    att_t_pair,
    ag32,
    ag,
    qg,
    kp,
    vp,
    halo_out,
    halo_in,
    out_stage,
    s1,
    r1,
    s2,
    r2,
    t1,
    p1,
    t2,
    p2,
    u,
    v,
    loc,
    sem_s,
    sem_r,
):
    ctx = lax.axis_index("ctx")
    fs = lax.axis_index("fsdp")
    z = ctx // 8
    y = (ctx // 2) % 4
    xl = ctx % 2
    xh = fs // 2
    core = fs % 2
    x = xh * 2 + xl
    n_ctx = 64

    def device(x_, y_, z_, core_):
        return (z_ * 8 + y_ * 2 + x_ % 2, (x_ // 2) * 2 + core_)

    pair = (ctx, xh * 2 + 1 - core)
    after = ((ctx + 1) % n_ctx, fs)
    before = ((ctx + n_ctx - 1) % n_ctx, fs)
    x_peer = [device(flip(x, m, 2), y, z, core) for m in (1, 2, 3)]
    y_peer = [device(x, flip(y, m, 2), z, core) for m in (1, 2, 3)]
    z_peer = [device(x, y, flip(z, m, 3), core) for m in range(1, 8)]
    z_step = {d: device(x, y, (z + d + 8) % 8, core) for d in (1, -1, 2, -2)}

    counter = [0]

    def remote(src, dst, target):
        index = counter[0]
        counter[0] += 1
        copy = pltpu.make_async_remote_copy(
            src_ref=src,
            dst_ref=dst,
            send_sem=sem_s.at[index],
            recv_sem=sem_r.at[index],
            device_id=target,
            device_id_type=MESH,
        )
        copy.start()
        started.append(copy)
        return copy

    started = []
    local_counter = [0]

    def local(src, dst):
        index = local_counter[0]
        local_counter[0] += 1
        copy = pltpu.make_async_copy(src, dst, loc.at[index])
        copy.start()
        return copy

    block = fs
    pair_block = xh * 2 + 1 - core
    far_block = (1 - xh) * 2 + core
    far_pair_block = (1 - xh) * 2 + 1 - core
    load_q = [local(query_hbm.at[:, pl.ds(i * GW, GW)], q_raw.at[i]) for i in range(GROUPS)]
    load_g = [local(grad_hbm.at[:, pl.ds(i * WIDTH, WIDTH)], g_own.at[i]) for i in range(4)]
    load_w = local(weight_hbm, w_all.at[block])

    barrier = pltpu.get_barrier_semaphore()
    greet = [pair, after, before] + x_peer + y_peer + z_peer
    for target in greet:
        pl.semaphore_signal(barrier, inc=1, device_id=target, device_id_type=MESH)

    lane_i = lax.broadcasted_iota(jnp.int32, (GW, GW), 0)
    lane_j = lax.broadcasted_iota(jnp.int32, (GW, GW), 1)
    first_j = lane_j % DH < HALF
    turn = jnp.where(
        first_j & (lane_i == lane_j + HALF),
        -1.0,
        jnp.where((~first_j) & (lane_i == lane_j - HALF), 1.0, 0.0),
    ).astype(BF)
    cos_k = jnp.concatenate([cos_ref[pl.ds(TOK, SPAN), :]] * 2, axis=1)
    sin_k = jnp.concatenate([sin_ref[pl.ds(TOK, SPAN), :]] * 2, axis=1)
    for i in range(GROUPS):
        sl = slice(i * GW, (i + 1) * GW)
        raw = key_ref[:, sl]
        turned = raw.astype(F32) * cos_k + dot(raw, turn, NN) * sin_k
        near_kv[0, :, sl] = jnp.concatenate([turned, value_ref[:, sl].astype(F32)], axis=0).astype(BF)

    pl.semaphore_wait(barrier, len(greet))

    halo_a = remote(near_kv.at[0], near_kv.at[1], after)
    halo_b = remote(near_kv.at[0], near_kv.at[2], before)
    quarter = z % 4
    cross = []
    for half in range(2):
        rows = pl.ds(quarter * 256 + half * 128, 128)
        cross.append(remote(weight_hbm.at[rows], w_all.at[block, rows], x_peer[2]))
    pair_g = [
        remote(
            grad_hbm.at[:, pl.ds(pl.multiple_of((2 * h + 1 - core) * WIDTH, WIDTH), WIDTH)],
            g_pair.at[h],
            pair,
        )
        for h in range(2)
    ]
    pair_w = remote(weight_hbm, w_all.at[block], pair)

    cos_q = jnp.concatenate([cos_ref[pl.ds(0, TOK), :]] * 2, axis=1)
    sin_q = jnp.concatenate([sin_ref[pl.ds(0, TOK), :]] * 2, axis=1)
    for copy in load_q:
        copy.wait()

    @pl.loop(0, GROUPS)
    def _(i):
        raw = q_raw[i]
        q_rot[i] = (raw.astype(F32) * cos_q + dot(raw, turn, NN) * sin_q).astype(BF)

    halo_a.wait_recv()
    halo_b.wait_recv()

    near_index = (
        lax.broadcasted_iota(jnp.int32, (NEAR, TOK), 0) + ctx * SPAN - SPAN
    )
    allowed = (near_index >= window_ref[0:1, :]) & (near_index < window_ref[1:2, :])
    head_row = lax.broadcasted_iota(jnp.int32, (GH, NEAR, GW), 0)
    head_col = lax.broadcasted_iota(jnp.int32, (GH, NEAR, GW), 2) // DH
    own_head = head_row == head_col

    def spread(row, i):
        sl = pl.ds(pl.multiple_of(i * GW, GW), GW)
        parts = [near_kv[slot, :, sl].astype(F32)[row : row + SPAN] for slot in (1, 0, 2)]
        near = jnp.concatenate(parts, axis=0)
        wide = jnp.where(own_head, near[None], 0.0)
        return wide.reshape(GH * NEAR, GW).astype(BF)

    def gather_heads(wide):
        shaped = wide.reshape(GH, NEAR, GW)
        return jnp.sum(jnp.where(own_head, shaped, 0.0), axis=0)

    @pl.loop(0, GROUPS)
    def _(i):
        keys = spread(0, i)
        values = spread(SPAN, i)
        scores = SCALE * dot(keys, q_rot[i], NT).reshape(GH, NEAR, TOK)
        masked = jnp.where(allowed[None], scores, -1e30)
        highest = jnp.max(masked, axis=1, keepdims=True)
        expo = jnp.where(allowed[None], jnp.exp(masked - highest), 0.0)
        probs = (expo / jnp.sum(expo, axis=1, keepdims=True)).reshape(GH * NEAR, TOK)
        probs_s[i] = probs
        low = probs.astype(BF)
        att[i] = dot(low, values, TN).astype(BF)
        att_t[pl.ds(pl.multiple_of(i * GW, GW), GW), :] = dot(values, low, TN).astype(BF)

    pair_a = remote(att_t, att_t_pair, pair)

    far_moves = []

    def pass_on(half):
        cross[half].wait_recv()
        rows = pl.ds(quarter * 256 + half * 128, 128)
        piece = w_all.at[far_block, rows]
        moves = [
            remote(piece, piece, z_step[1]),
            remote(piece, piece, z_step[-1]),
            remote(piece, piece, z_step[2 if half == 0 else -2]),
            remote(piece, piece, pair),
        ]
        far_moves.append(moves)

    pass_on(0)

    for copy in load_g:
        copy.wait()
    for copy in pair_g:
        copy.wait_recv()
    pair_a.wait_recv()

    def gradient(h, part, store):
        cols = slice(part * 512, (part + 1) * 512)

        @pl.loop(0, 2)
        def _(i):
            rows = pl.ds(pl.multiple_of(i * 512, 512), 512)
            total = dot(att_t[rows, :], g_own[2 * h + core, :, cols], NN)
            total = total + dot(att_t_pair[rows, :], g_pair[h, :, cols], NN)
            store(i, total.astype(BF).reshape(4, 4, 2, 16, 512))

    def store_x(h):
        def store(i, total):
            for low_x in range(2):
                s1[2 * h + low_x, pl.ds(i * 4, 4)] = total[:, :, low_x]

        return store

    def store_y(h):
        def store(i, total):
            for to_y in range(4):
                s2[to_y, h, pl.ds(i * 4, 4)] = total[:, to_y]

        return store

    x_moves = {}

    def send_x(m):
        x_moves[m] = remote(s1.at[flip(x, m, 2)], r1.at[m - 1], x_peer[m - 1])

    y_moves = {}

    def send_y(m, h):
        y_moves[m, h] = remote(s2.at[flip(y, m, 2), h], r2.at[m - 1, h], y_peer[m - 1])

    gradient(1 - xh, 0, store_x(1 - xh))
    send_x(2)
    send_x(3)
    gradient(0, 1, store_y(0))
    for m in (1, 2, 3):
        send_y(m, 0)
    gradient(xh, 0, store_x(xh))
    send_x(1)
    pass_on(1)
    gradient(1, 1, store_y(1))
    for m in (1, 2, 3):
        send_y(m, 1)

    load_w.wait()
    pair_w.wait_recv()

    out_moves = []

    def project(b):
        @pl.loop(0, 2)
        def _(j):
            cols = pl.ds(pl.multiple_of(j * 512, 512), 512)
            total = dot(att[0], w_all[b, 0:GW, cols], NN)
            for i in range(1, GROUPS):
                total = total + dot(att[i], w_all[b, i * GW : (i + 1) * GW, cols], NN)
            out_stage[b, :, cols] = total.astype(BF)

        out_moves.append(
            local(out_stage.at[b], out_hbm.at[:, pl.ds(pl.multiple_of(b * WIDTH, WIDTH), WIDTH)])
        )

    @pl.loop(0, 2)
    def _(j):
        rows = pl.ds(pl.multiple_of(j * 512, 512), 512)
        ag32[j] = dot(g_own[block], w_all[block, rows, :], NT) + dot(
            g_own[pair_block], w_all[pair_block, rows, :], NT
        )

    project(block)
    project(pair_block)

    for half in range(2):
        rows = [
            pl.ds(((z + 3) % 4) * 256 + half * 128, 128),
            pl.ds(((z + 1) % 4) * 256 + half * 128, 128),
            pl.ds(((z + 2) % 4) * 256 + half * 128, 128),
        ]
        for k in range(3):
            far_moves[half][k].wait_recv()
            piece = w_all.at[far_block, rows[k]]
            far_moves[half].append(remote(piece, piece, pair))

    for m in (1, 2, 3):
        x_moves[m].wait_recv()

    @pl.loop(0, 4)
    def _(to_y):
        total = s1[x, :, to_y].astype(F32)
        for m in range(3):
            total = total + r1[m, :, to_y].astype(F32)
        t1[to_y] = total.astype(BF)

    y2_moves = [remote(t1.at[flip(y, m, 2)], p1.at[m - 1], y_peer[m - 1]) for m in (1, 2, 3)]
    for m in (1, 2, 3):
        for h in range(2):
            y_moves[m, h].wait_recv()

    @pl.loop(0, 4)
    def _(to_x):
        h = to_x // 2
        low_x = to_x % 2
        total = s2[y, h, :, low_x].astype(F32)
        for m in range(3):
            total = total + r2[m, h, :, low_x].astype(F32)
        t2[to_x] = total.astype(BF)

    x2_moves = [remote(t2.at[flip(x, m, 2)], p2.at[m - 1], x_peer[m - 1]) for m in (1, 2, 3)]

    for half in range(2):
        for k in range(3, 7):
            far_moves[half][k].wait_recv()

    @pl.loop(0, 2)
    def _(j):
        rows = pl.ds(pl.multiple_of(j * 512, 512), 512)
        total = ag32[j] + dot(g_own[far_block], w_all[far_block, rows, :], NT)
        total = total + dot(g_own[far_pair_block], w_all[far_pair_block, rows, :], NT)
        low = total.astype(BF)
        ag[2 * j] = low[:, :GW]
        ag[2 * j + 1] = low[:, GW:]

    @pl.loop(0, GROUPS)
    def _(i):
        keys = spread(0, i)
        values = spread(SPAN, i)
        grads = ag[i]
        probs = probs_s[i]
        low = probs.astype(BF)
        sl = pl.ds(pl.multiple_of(i * GW, GW), GW)
        vp[:, sl] = gather_heads(dot(low, grads, NN))
        shaped = probs.reshape(GH, NEAR, TOK)
        prob_grad = dot(values, grads, NT).reshape(GH, NEAR, TOK)
        row_dot = jnp.sum(shaped * prob_grad, axis=1, keepdims=True)
        score_grad = (shaped * (prob_grad - row_dot)).reshape(GH * NEAR, TOK).astype(BF)
        turned_keys = dot(keys, turn, NN).astype(BF)
        part = SCALE * dot(score_grad, keys, TN)
        part_turned = SCALE * dot(score_grad, turned_keys, TN)
        qg[i] = (part * cos_q - part_turned * sin_q).astype(BF)
        kp[:, sl] = gather_heads(SCALE * dot(score_grad, q_rot[i], NN))

    halo_out[0, 0:SPAN] = kp[2 * SPAN :, :]
    halo_out[0, SPAN:] = vp[2 * SPAN :, :]
    halo_out[1, 0:SPAN] = kp[0:SPAN, :]
    halo_out[1, SPAN:] = vp[0:SPAN, :]
    back = [
        remote(halo_out.at[0], halo_in.at[0], after),
        remote(halo_out.at[1], halo_in.at[1], before),
    ]
    for i in range(GROUPS):
        out_moves.append(local(qg.at[i], qgrad_hbm.at[:, pl.ds(i * GW, GW)]))

    project(far_block)

    for copy in y2_moves + x2_moves:
        copy.wait_recv()
    first = t1[y].astype(F32)
    second = t2[x].astype(F32)
    for m in range(3):
        first = first + p1[m].astype(F32)
        second = second + p2[m].astype(F32)
    u[:, :, 0:512] = first.astype(BF)
    u[:, :, 512:1024] = second.astype(BF)
    z_moves = [remote(u.at[flip(z, m, 3)], v.at[m - 1], z_peer[m - 1]) for m in range(1, 8)]

    project(far_pair_block)

    for copy in back:
        copy.wait_recv()
    vgrad_ref[...] = vp[SPAN : 2 * SPAN, :] + halo_in[0, SPAN:] + halo_in[1, SPAN:]
    key_total = kp[SPAN : 2 * SPAN, :] + halo_in[0, 0:SPAN] + halo_in[1, 0:SPAN]
    lane = lax.broadcasted_iota(jnp.int32, (SPAN, WIDTH), 1) % DH
    other = jnp.where(
        lane < HALF,
        -pltpu.roll(key_total, WIDTH - HALF, 1),
        pltpu.roll(key_total, HALF, 1),
    )
    wide_cos = jnp.concatenate([cos_k] * GROUPS, axis=1)
    wide_sin = jnp.concatenate([sin_k] * GROUPS, axis=1)
    kgrad_ref[...] = key_total * wide_cos - other * wide_sin

    for copy in z_moves:
        copy.wait_recv()
    total = u[z].astype(F32)
    for m in range(7):
        total = total + v[m].astype(F32)
    wgrad_ref[...] = total * factor

    for copy in out_moves:
        copy.wait()
    for copy in started:
        copy.wait_send()


def local(video_query, audio_key, audio_value, out_weight, grad_out, query_time, window):
    shard = lax.axis_index("ctx")
    freqs = np.tile((10000.0 ** (-np.arange(HALF) / HALF)).astype(np.float32), 128 // HALF)
    key_index = shard * SPAN + jnp.arange(SPAN, dtype=jnp.int32)
    positions = jnp.concatenate([query_time, key_index]).astype(F32)
    angles = positions[:, None] * freqs[None, :]
    factor = 1.0 / math.sqrt(TOK * lax.axis_size("ctx") * lax.axis_size("fsdp"))

    vmem = pl.BlockSpec(memory_space=pltpu.VMEM)
    hbm = pl.BlockSpec(memory_space=pl.ANY)
    n_sems = 48

    def body(*refs):
        kernel(factor, *refs)

    outs = pl.pallas_call(
        body,
        name="fused",
        out_shape=(
            jax.ShapeDtypeStruct((TOK, 4 * WIDTH), BF),
            jax.ShapeDtypeStruct((TOK, WIDTH), BF),
            jax.ShapeDtypeStruct((SPAN, WIDTH), F32),
            jax.ShapeDtypeStruct((SPAN, WIDTH), F32),
            jax.ShapeDtypeStruct((16, WIDTH), F32),
        ),
        in_specs=[hbm, vmem, vmem, hbm, hbm, vmem, vmem, vmem],
        out_specs=(hbm, hbm, vmem, vmem, vmem),
        scratch_shapes=[
            pltpu.VMEM((GROUPS, TOK, GW), BF),
            pltpu.VMEM((GROUPS, TOK, GW), BF),
            pltpu.VMEM((3, 2 * SPAN, WIDTH), BF),
            pltpu.VMEM((4, WIDTH, WIDTH), BF),
            pltpu.VMEM((4, TOK, WIDTH), BF),
            pltpu.VMEM((2, TOK, WIDTH), BF),
            pltpu.VMEM((GROUPS, GH * NEAR, TOK), F32),
            pltpu.VMEM((GROUPS, TOK, GW), BF),
            pltpu.VMEM((WIDTH, TOK), BF),
            pltpu.VMEM((WIDTH, TOK), BF),
            pltpu.VMEM((2, TOK, 512), F32),
            pltpu.VMEM((GROUPS, TOK, GW), BF),
            pltpu.VMEM((GROUPS, TOK, GW), BF),
            pltpu.VMEM((NEAR, WIDTH), F32),
            pltpu.VMEM((NEAR, WIDTH), F32),
            pltpu.VMEM((2, 2 * SPAN, WIDTH), F32),
            pltpu.VMEM((2, 2 * SPAN, WIDTH), F32),
            pltpu.VMEM((4, TOK, WIDTH), BF),
            pltpu.VMEM((4, 8, 4, 16, 512), BF),
            pltpu.VMEM((3, 8, 4, 16, 512), BF),
            pltpu.VMEM((4, 2, 8, 2, 16, 512), BF),
            pltpu.VMEM((3, 2, 8, 2, 16, 512), BF),
            pltpu.VMEM((4, 8, 16, 512), BF),
            pltpu.VMEM((3, 8, 16, 512), BF),
            pltpu.VMEM((4, 8, 16, 512), BF),
            pltpu.VMEM((3, 8, 16, 512), BF),
            pltpu.VMEM((8, 16, WIDTH), BF),
            pltpu.VMEM((7, 16, WIDTH), BF),
            pltpu.SemaphoreType.DMA((24,)),
            pltpu.SemaphoreType.DMA((n_sems,)),
            pltpu.SemaphoreType.DMA((n_sems,)),
        ],
        compiler_params=pltpu.CompilerParams(
            collective_id=0, has_side_effects=True, vmem_limit_bytes=58 << 20
        ),
    )(
        video_query[0],
        audio_key[0],
        audio_value[0],
        out_weight,
        grad_out[0],
        jnp.cos(angles),
        jnp.sin(angles),
        window,
    )
    output, query_grad, key_grad, value_grad, weight_grad = outs
    return (output[None], query_grad[None], key_grad[None], value_grad[None], weight_grad)


def solution(mesh):
    in_specs = (
        P("fsdp", "ctx", None),
        P("fsdp", "ctx", None),
        P("fsdp", "ctx", None),
        P(None, "fsdp"),
        P("fsdp", "ctx", None),
        P("ctx"),
        P(None, "ctx"),
    )
    out_specs = (
        P("fsdp", "ctx", None),
        P("fsdp", "ctx", None),
        P("fsdp", "ctx", None),
        P("fsdp", "ctx", None),
        P("ctx", "fsdp"),
    )
    return jax.shard_map(local, mesh=mesh, in_specs=in_specs, out_specs=out_specs, check_vma=False)
```

time: 476 us -> 78.2 us (0.16)
  the two profiles are of different devices: /device:TPU:4 before, /device:TPU:1 now
where the time goes in v1:
time: 78.2 us; the launch traced here: 78 us
  Pallas kernels  66.5 us (85%)
  local copies, waits for them, and re-layouts  7.63 us (10%)
  other arithmetic  3.19 us (4%)
    pallas_call x1, Pallas kernels, local(): pl.pallas_call(body, name='fused', out_shape=(jax.ShapeDtypeStruct((TOK,...  66.5 us
    unnamed x13, local copies, waits for them, and re-layouts  7.63 us
    sin x1, other arithmetic, local(): jnp.sin(angles)  2.49 us

profile of v1, /device:TPU:1, one launch (start us, length us, event | category | flops | bytes accessed | tf_op | source)
XLA Modules:
  0.0 78.0 jit_solution(16336213868152915416)
XLA Ops:
  0.6 0.7 add_convert_fusion
  1.3 2.5 %multiply_sine_fusion = (f32[520,128]{1,0:T(8,128)}, f32[520,128]{1,0:T(8,128)}) fusion(f32[128]{0:T(128)} %constant.15, f32[520]{0:T(1024)S(1)} %add_convert_fusion), kind=kLoop, calls=%fused_computation | loop fusion | flops 66560 | bytes 535072 | tf_op jit(solution)/shard_map/sin | solution.py:524
  3.8 66.5 %fused.1 = (bf16[512,4096]{1,0:T(8,128)(2,1)}, bf16[512,1024]{1,0:T(8,128)(2,1)}, f32[8,1024]{1,0:T(8,128)}, f32[8,1024]{1,0:T(8,128)}, f32[16,1024]{1,0:T(8,128)}) custom-call(bf16[512,1024]{1,0:T(8,128)(2,1)} %bitcast.10, bf16[8,1024]{1,0:T(8,128)(2,1)} %bitcast.14, bf16[8,1024]{1,0:T(8,128)(2,1)} %bitcast.15, bf16[1024,1024]{1,0:T(8,128)(2,1)} %refs_3_.1, ...), custom_call_target="tpu_custom_call" | custom-call | tf_op jit(solution)/shard_map/fused/pallas_call | solution.py:469
  70.4 0.0 copy-start
  70.4 0.0 copy-start.3
  70.4 0.0 copy-start.2
  70.4 0.0 copy-start.1
  70.4 4.8 %copy.18 = bf16[1,512,4096]{2,1,0:T(8,128)(2,1)} copy(bf16[1,512,4096]{2,1,0:T(8,128)(2,1)} %bitcast.9) | data formatting | bytes 8388608
  75.2 0.0 copy-done
  75.2 1.0 %copy.19 = bf16[1,512,1024]{2,1,0:T(8,128)(2,1)} copy(bf16[1,512,1024]{2,1,0:T(8,128)(2,1)S(1)} %bitcast.11) | data formatting | bytes 2097152
  76.1 0.0 copy-done.3
  76.2 0.6 copy.20
  76.8 0.0 copy-done.2
  76.8 0.6 copy.21
  77.4 0.0 copy-done.1
  77.4 0.6 copy.22
  (1 shorter events, 0.0 us)
Async XLA Ops:
  70.4 4.8 %copy-start = (bf16[512,1024]{1,0:T(8,128)(2,1)S(1)}, bf16[512,1024]{1,0:T(8,128)(2,1)}, u32[]{:S(2)}) copy-start(bf16[512,1024]{1,0:T(8,128)(2,1)} %get-tuple-element.11) | copy-start | bytes 3145732
  70.4 5.8 %copy-start.3 = (f32[8,1024]{1,0:T(8,128)S(1)}, f32[8,1024]{1,0:T(8,128)}, u32[]{:S(2)}) copy-start(f32[8,1024]{1,0:T(8,128)} %get-tuple-element.12) | copy-start | bytes 98308
  70.4 6.4 %copy-start.2 = (f32[8,1024]{1,0:T(8,128)S(1)}, f32[8,1024]{1,0:T(8,128)}, u32[]{:S(2)}) copy-start(f32[8,1024]{1,0:T(8,128)} %get-tuple-element.13) | copy-start | bytes 98308
  70.4 7.0 %copy-start.1 = (f32[16,1024]{1,0:T(8,128)S(1)}, f32[16,1024]{1,0:T(8,128)}, u32[]{:S(2)}) copy-start(f32[16,1024]{1,0:T(8,128)} %get-tuple-element.26) | copy-start | bytes 196612

commit v2 on v1

--- a/solution.py
+++ b/solution.py
@@ -48,11 +48,11 @@
     value_ref,
     weight_hbm,
     grad_hbm,
-    cos_ref,
-    sin_ref,
+    time_ref,
     window_ref,
-    out_hbm,
-    qgrad_hbm,
+    freq_ref,
+    out_stage,
+    qgrad,
     kgrad_ref,
     vgrad_ref,
     wgrad_ref,
@@ -68,12 +68,11 @@
     att_t_pair,
     ag32,
     ag,
-    qg,
+    table,
     kp,
     vp,
     halo_out,
     halo_in,
-    out_stage,
     s1,
     r1,
     s2,
@@ -157,8 +156,27 @@
         -1.0,
         jnp.where((~first_j) & (lane_i == lane_j - HALF), 1.0, 0.0),
     ).astype(BF)
-    cos_k = jnp.concatenate([cos_ref[pl.ds(TOK, SPAN), :]] * 2, axis=1)
-    sin_k = jnp.concatenate([sin_ref[pl.ds(TOK, SPAN), :]] * 2, axis=1)
+    near_row = lax.broadcasted_iota(jnp.int32, (32, 1), 0) + ctx * SPAN - SPAN
+    angles = near_row.astype(F32) * freq_ref[...]
+    near_table = jnp.concatenate([jnp.cos(angles), jnp.sin(angles)], axis=1)
+    pieces = []
+    rest = near_table
+    for _ in range(3):
+        piece = rest.astype(BF).astype(F32)
+        pieces.append(piece)
+        rest = rest - piece
+    time_row = jnp.where(near_row == time_ref[...], 1.0, 0.0)
+    chosen = jnp.concatenate([time_row] * 3, axis=0).astype(BF)
+    table[...] = dot(chosen, jnp.concatenate(pieces, axis=0).astype(BF), TN)
+
+    def cos_q():
+        return jnp.concatenate([table[:, :128]] * 2, axis=1)
+
+    def sin_q():
+        return jnp.concatenate([table[:, 128:]] * 2, axis=1)
+
+    cos_k = jnp.concatenate([near_table[SPAN : 2 * SPAN, :128]] * 2, axis=1)
+    sin_k = jnp.concatenate([near_table[SPAN : 2 * SPAN, 128:]] * 2, axis=1)
     for i in range(GROUPS):
         sl = slice(i * GW, (i + 1) * GW)
         raw = key_ref[:, sl]
@@ -182,17 +200,23 @@
         )
         for h in range(2)
     ]
-    pair_w = remote(weight_hbm, w_all.at[block], pair)
-
-    cos_q = jnp.concatenate([cos_ref[pl.ds(0, TOK), :]] * 2, axis=1)
-    sin_q = jnp.concatenate([sin_ref[pl.ds(0, TOK), :]] * 2, axis=1)
+
     for copy in load_q:
         copy.wait()
 
     @pl.loop(0, GROUPS)
     def _(i):
         raw = q_raw[i]
-        q_rot[i] = (raw.astype(F32) * cos_q + dot(raw, turn, NN) * sin_q).astype(BF)
+        q_rot[i] = (raw.astype(F32) * cos_q() + dot(raw, turn, NN) * sin_q()).astype(BF)
+
+    def early(j):
+        rows = pl.ds(j * 512, 512)
+        ag32[j] = dot(g_own[block], w_all[block, rows, :], NT)
+
+    for copy in load_g:
+        copy.wait()
+    load_w.wait()
+    early(0)
 
     halo_a.wait_recv()
     halo_b.wait_recv()
@@ -216,8 +240,8 @@
         shaped = wide.reshape(GH, NEAR, GW)
         return jnp.sum(jnp.where(own_head, shaped, 0.0), axis=0)
 
-    @pl.loop(0, GROUPS)
-    def _(i):
+    pair_a = []
+    for i in range(GROUPS):
         keys = spread(0, i)
         values = spread(SPAN, i)
         scores = SCALE * dot(keys, q_rot[i], NT).reshape(GH, NEAR, TOK)
@@ -227,10 +251,13 @@
         probs = (expo / jnp.sum(expo, axis=1, keepdims=True)).reshape(GH * NEAR, TOK)
         probs_s[i] = probs
         low = probs.astype(BF)
+        rows = pl.ds(i * GW, GW)
+        att_t[rows, :] = dot(values, low, TN).astype(BF)
+        pair_a.append(remote(att_t.at[rows], att_t_pair.at[rows], pair))
         att[i] = dot(low, values, TN).astype(BF)
-        att_t[pl.ds(pl.multiple_of(i * GW, GW), GW), :] = dot(values, low, TN).astype(BF)
-
-    pair_a = remote(att_t, att_t_pair, pair)
+
+    pair_w = remote(weight_hbm, w_all.at[block], pair)
+    early(1)
 
     far_moves = []
 
@@ -246,13 +273,8 @@
         ]
         far_moves.append(moves)
 
-    pass_on(0)
-
-    for copy in load_g:
-        copy.wait()
-    for copy in pair_g:
+    for copy in pair_g + pair_a:
         copy.wait_recv()
-    pair_a.wait_recv()
 
     def gradient(h, part, store):
         cols = slice(part * 512, (part + 1) * 512)
@@ -267,64 +289,87 @@
     def store_x(h):
         def store(i, total):
             for low_x in range(2):
-                s1[2 * h + low_x, pl.ds(i * 4, 4)] = total[:, :, low_x]
+                for k in range(2):
+                    s1[2 * h + low_x, k, pl.ds(i * 4, 4)] = total[:, :, low_x, :, k * 256 : k * 256 + 256]
 
         return store
 
     def store_y(h):
         def store(i, total):
             for to_y in range(4):
-                s2[to_y, h, pl.ds(i * 4, 4)] = total[:, to_y]
+                for k in range(2):
+                    s2[to_y, k, h, pl.ds(i * 4, 4)] = total[:, to_y, :, :, k * 256 : k * 256 + 256]
 
         return store
 
-    x_moves = {}
-
-    def send_x(m):
-        x_moves[m] = remote(s1.at[flip(x, m, 2)], r1.at[m - 1], x_peer[m - 1])
-
-    y_moves = {}
-
-    def send_y(m, h):
-        y_moves[m, h] = remote(s2.at[flip(y, m, 2), h], r2.at[m - 1, h], y_peer[m - 1])
+    near = (1, 3)
+    x_first = {}
+    y_first = {}
+
+    def send_x(k, slot):
+        to = flip(x, 2 if slot == 0 else near[k], 2)
+        x_first[k, slot] = remote(s1.at[to, k], r1.at[k, slot], x_peer[near[k] - 1])
+
+    def send_y(k, slot, h):
+        to = flip(y, 2 if slot == 0 else near[k], 2)
+        y_first[k, slot, h] = remote(s2.at[to, k, h], r2.at[k, slot, h], y_peer[near[k] - 1])
 
     gradient(1 - xh, 0, store_x(1 - xh))
-    send_x(2)
-    send_x(3)
-    gradient(0, 1, store_y(0))
-    for m in (1, 2, 3):
-        send_y(m, 0)
+    send_x(1, 0)
+    send_x(0, 0)
+    send_x(1, 1)
+    pass_on(0)
+    for h in range(2):
+        gradient(h, 1, store_y(h))
+        for slot in range(2):
+            for k in range(2):
+                send_y(k, slot, h)
     gradient(xh, 0, store_x(xh))
-    send_x(1)
+    send_x(0, 1)
     pass_on(1)
-    gradient(1, 1, store_y(1))
-    for m in (1, 2, 3):
-        send_y(m, 1)
-
-    load_w.wait()
+
+    x_second = []
+    y_second = []
+    for k in range(2):
+        to = flip(x, near[1 - k], 2)
+        x_first[k, 0].wait_recv()
+
+        @pl.loop(0, 4)
+        def _(i):
+            part = pl.ds(i * 2, 2)
+            s1[to, k, part] = (s1[to, k, part].astype(F32) + r1[k, 0, part].astype(F32)).astype(BF)
+
+        x_second.append(remote(s1.at[to, k], r1.at[k, 2], x_peer[near[1 - k] - 1]))
+    for k in range(2):
+        to = flip(y, near[1 - k], 2)
+        for h in range(2):
+            y_first[k, 0, h].wait_recv()
+
+            @pl.loop(0, 2)
+            def _(i):
+                part = pl.ds(i * 4, 4)
+                s2[to, k, h, part] = (
+                    s2[to, k, h, part].astype(F32) + r2[k, 0, h, part].astype(F32)
+                ).astype(BF)
+
+        y_second.append(remote(s2.at[to, k], r2.at[k, 2], y_peer[near[1 - k] - 1]))
+
     pair_w.wait_recv()
-
-    out_moves = []
 
     def project(b):
         @pl.loop(0, 2)
         def _(j):
             cols = pl.ds(pl.multiple_of(j * 512, 512), 512)
+            out_cols = pl.ds(pl.multiple_of(b * WIDTH + j * 512, 512), 512)
             total = dot(att[0], w_all[b, 0:GW, cols], NN)
             for i in range(1, GROUPS):
                 total = total + dot(att[i], w_all[b, i * GW : (i + 1) * GW, cols], NN)
-            out_stage[b, :, cols] = total.astype(BF)
-
-        out_moves.append(
-            local(out_stage.at[b], out_hbm.at[:, pl.ds(pl.multiple_of(b * WIDTH, WIDTH), WIDTH)])
-        )
+            out_stage[:, out_cols] = total.astype(BF)
 
     @pl.loop(0, 2)
     def _(j):
         rows = pl.ds(pl.multiple_of(j * 512, 512), 512)
-        ag32[j] = dot(g_own[block], w_all[block, rows, :], NT) + dot(
-            g_own[pair_block], w_all[pair_block, rows, :], NT
-        )
+        ag32[j] += dot(g_own[pair_block], w_all[pair_block, rows, :], NT)
 
     project(block)
     project(pair_block)
@@ -340,29 +385,33 @@
             piece = w_all.at[far_block, rows[k]]
             far_moves[half].append(remote(piece, piece, pair))
 
-    for m in (1, 2, 3):
-        x_moves[m].wait_recv()
+    for k in range(2):
+        x_first[k, 1].wait_recv()
+        x_second[k].wait_recv()
 
     @pl.loop(0, 4)
     def _(to_y):
-        total = s1[x, :, to_y].astype(F32)
-        for m in range(3):
-            total = total + r1[m, :, to_y].astype(F32)
-        t1[to_y] = total.astype(BF)
+        for k in range(2):
+            total = s1[x, k, :, to_y].astype(F32)
+            for m in (1, 2):
+                total = total + r1[k, m, :, to_y].astype(F32)
+            t1[to_y, :, :, k * 256 : k * 256 + 256] = total.astype(BF)
 
     y2_moves = [remote(t1.at[flip(y, m, 2)], p1.at[m - 1], y_peer[m - 1]) for m in (1, 2, 3)]
-    for m in (1, 2, 3):
+    for k in range(2):
         for h in range(2):
-            y_moves[m, h].wait_recv()
+            y_first[k, 1, h].wait_recv()
+        y_second[k].wait_recv()
 
     @pl.loop(0, 4)
     def _(to_x):
         h = to_x // 2
         low_x = to_x % 2
-        total = s2[y, h, :, low_x].astype(F32)
-        for m in range(3):
-            total = total + r2[m, h, :, low_x].astype(F32)
-        t2[to_x] = total.astype(BF)
+        for k in range(2):
+            total = s2[y, k, h, :, low_x].astype(F32)
+            for m in (1, 2):
+                total = total + r2[k, m, h, :, low_x].astype(F32)
+            t2[to_x, :, :, k * 256 : k * 256 + 256] = total.astype(BF)
 
     x2_moves = [remote(t2.at[flip(x, m, 2)], p2.at[m - 1], x_peer[m - 1]) for m in (1, 2, 3)]
 
@@ -395,7 +444,7 @@
         turned_keys = dot(keys, turn, NN).astype(BF)
         part = SCALE * dot(score_grad, keys, TN)
         part_turned = SCALE * dot(score_grad, turned_keys, TN)
-        qg[i] = (part * cos_q - part_turned * sin_q).astype(BF)
+        qgrad[:, sl] = (part * cos_q() - part_turned * sin_q()).astype(BF)
         kp[:, sl] = gather_heads(SCALE * dot(score_grad, q_rot[i], NN))
 
     halo_out[0, 0:SPAN] = kp[2 * SPAN :, :]
@@ -406,8 +455,6 @@
         remote(halo_out.at[0], halo_in.at[0], after),
         remote(halo_out.at[1], halo_in.at[1], before),
     ]
-    for i in range(GROUPS):
-        out_moves.append(local(qg.at[i], qgrad_hbm.at[:, pl.ds(i * GW, GW)]))
 
     project(far_block)
 
@@ -445,23 +492,33 @@
         total = total + v[m].astype(F32)
     wgrad_ref[...] = total * factor
 
-    for copy in out_moves:
-        copy.wait()
     for copy in started:
         copy.wait_send()
 
 
+def finish(*refs):
+    sems = refs[10]
+    copies = [pltpu.make_async_copy(refs[i], refs[5 + i], sems.at[i]) for i in range(5)]
+    for copy in copies:
+        copy.start()
+    for copy in copies:
+        copy.wait()
+
+
 def local(video_query, audio_key, audio_value, out_weight, grad_out, query_time, window):
-    shard = lax.axis_index("ctx")
     freqs = np.tile((10000.0 ** (-np.arange(HALF) / HALF)).astype(np.float32), 128 // HALF)
-    key_index = shard * SPAN + jnp.arange(SPAN, dtype=jnp.int32)
-    positions = jnp.concatenate([query_time, key_index]).astype(F32)
-    angles = positions[:, None] * freqs[None, :]
     factor = 1.0 / math.sqrt(TOK * lax.axis_size("ctx") * lax.axis_size("fsdp"))
 
     vmem = pl.BlockSpec(memory_space=pltpu.VMEM)
     hbm = pl.BlockSpec(memory_space=pl.ANY)
-    n_sems = 48
+    n_sems = 56
+    results = [
+        ((TOK, 4 * WIDTH), BF),
+        ((TOK, WIDTH), BF),
+        ((SPAN, WIDTH), F32),
+        ((SPAN, WIDTH), F32),
+        ((16, WIDTH), F32),
+    ]
 
     def body(*refs):
         kernel(factor, *refs)
@@ -469,15 +526,9 @@
     outs = pl.pallas_call(
         body,
         name="fused",
-        out_shape=(
-            jax.ShapeDtypeStruct((TOK, 4 * WIDTH), BF),
-            jax.ShapeDtypeStruct((TOK, WIDTH), BF),
-            jax.ShapeDtypeStruct((SPAN, WIDTH), F32),
-            jax.ShapeDtypeStruct((SPAN, WIDTH), F32),
-            jax.ShapeDtypeStruct((16, WIDTH), F32),
-        ),
+        out_shape=[pltpu.VMEM(shape, dtype) for shape, dtype in results],
         in_specs=[hbm, vmem, vmem, hbm, hbm, vmem, vmem, vmem],
-        out_specs=(hbm, hbm, vmem, vmem, vmem),
+        out_specs=[vmem] * 5,
         scratch_shapes=[
             pltpu.VMEM((GROUPS, TOK, GW), BF),
             pltpu.VMEM((GROUPS, TOK, GW), BF),
@@ -491,16 +542,15 @@
             pltpu.VMEM((WIDTH, TOK), BF),
             pltpu.VMEM((2, TOK, 512), F32),
             pltpu.VMEM((GROUPS, TOK, GW), BF),
-            pltpu.VMEM((GROUPS, TOK, GW), BF),
+            pltpu.VMEM((TOK, 256), F32),
             pltpu.VMEM((NEAR, WIDTH), F32),
             pltpu.VMEM((NEAR, WIDTH), F32),
             pltpu.VMEM((2, 2 * SPAN, WIDTH), F32),
             pltpu.VMEM((2, 2 * SPAN, WIDTH), F32),
-            pltpu.VMEM((4, TOK, WIDTH), BF),
-            pltpu.VMEM((4, 8, 4, 16, 512), BF),
-            pltpu.VMEM((3, 8, 4, 16, 512), BF),
-            pltpu.VMEM((4, 2, 8, 2, 16, 512), BF),
-            pltpu.VMEM((3, 2, 8, 2, 16, 512), BF),
+            pltpu.VMEM((4, 2, 8, 4, 16, 256), BF),
+            pltpu.VMEM((2, 3, 8, 4, 16, 256), BF),
+            pltpu.VMEM((4, 2, 2, 8, 2, 16, 256), BF),
+            pltpu.VMEM((2, 3, 2, 8, 2, 16, 256), BF),
             pltpu.VMEM((4, 8, 16, 512), BF),
             pltpu.VMEM((3, 8, 16, 512), BF),
             pltpu.VMEM((4, 8, 16, 512), BF),
@@ -512,7 +562,7 @@
             pltpu.SemaphoreType.DMA((n_sems,)),
         ],
         compiler_params=pltpu.CompilerParams(
-            collective_id=0, has_side_effects=True, vmem_limit_bytes=58 << 20
+            collective_id=0, has_side_effects=True, vmem_limit_bytes=46 << 20
         ),
     )(
         video_query[0],
@@ -520,10 +570,18 @@
         audio_value[0],
         out_weight,
         grad_out[0],
-        jnp.cos(angles),
-        jnp.sin(angles),
+        query_time.reshape(1, TOK),
         window,
+        jnp.asarray(freqs).reshape(1, 128),
     )
+    outs = pl.pallas_call(
+        finish,
+        name="finish",
+        out_shape=[jax.ShapeDtypeStruct(shape, dtype) for shape, dtype in results],
+        in_specs=[vmem] * 5,
+        out_specs=[hbm] * 5,
+        scratch_shapes=[pltpu.SemaphoreType.DMA((5,))],
+    )(*outs)
     output, query_grad, key_grad, value_grad, weight_grad = outs
     return (output[None], query_grad[None], key_grad[None], value_grad[None], weight_grad)
 

time: 78.2 us -> 78.5 us (level)
  the two profiles are of different devices: /device:TPU:1 before, /device:TPU:4 now
where the time goes in v2:
time: 78.5 us; the launch traced here: 77.7 us
  Pallas kernels  67.6 us (86%)
  local copies, waits for them, and re-layouts  9.44 us (12%)
    pallas_call x1, Pallas kernels, local(): pl.pallas_call(body, name='fused', out_shape=[pltpu.VMEM(shape, dtype) fo...  62.6 us
    unnamed x22, local copies, waits for them, and re-layouts  9.44 us
    pallas_call x1, Pallas kernels, local(): pl.pallas_call(finish, name='finish', out_shape=[jax.ShapeDtypeStruct(sha...  4.93 us

profile of v2, /device:TPU:4, one launch (start us, length us, event | category | flops | bytes accessed | tf_op | source)
XLA Modules:
  0.0 77.7 jit_solution(8128055407727817742)
XLA Ops:
  0.6 0.0 copy-start.1
  0.6 1.2 %copy-done.1 = bf16[1,512,1024]{2,1,0:T(8,128)(2,1)S(1)} copy-done((bf16[1,512,1024]{2,1,0:T(8,128)(2,1)S(1)}, bf16[1,512,1024]{2,1,0:T(8,128)(2,1)}, u32[]{:S(2)}) %copy-start.1) | copy-done | bytes 1048600
  1.9 0.0 copy-start.6
  1.9 0.7 copy-done.6
  2.6 0.0 copy-start.7
  2.6 0.7 copy-done.7
  3.3 0.0 copy-start.8
  3.3 0.7 copy-done.8
  4.0 0.0 copy-start.9
  4.0 0.7 copy-done.9
  4.7 0.0 copy-start.10
  4.7 0.7 copy-done.10
  5.3 62.6 %fused.1 = (bf16[512,4096]{1,0:T(8,128)(2,1)S(1)}, bf16[512,1024]{1,0:T(8,128)(2,1)S(1)}, f32[8,1024]{1,0:T(8,128)S(1)}, f32[8,1024]{1,0:T(8,128)S(1)}, f32[16,1024]{1,0:T(8,128)S(1)}) custom-call(bf16[512,1024]{1,0:T(8,128)(2,1)S(1)} %bitcast.9, bf16[8,1024]{1,0:T(8,128)(2,1)S(1)} %bitcast.10, bf16[8,1024]{1,0:T(8,128)(2,1)S(1)} %bitcast.11, ...), custom_call_target="tpu_custom_call" | custom-call | tf_op jit(solution)/shard_map/fused/pallas_call | solution.py:526
  68.0 0.0 copy-start
  68.0 1.9 %copy-done = bf16[512,4096]{1,0:T(8,128)(2,1)} copy-done((bf16[512,4096]{1,0:T(8,128)(2,1)}, bf16[512,4096]{1,0:T(8,128)(2,1)S(1)}, u32[]{:S(2)}) %copy-start) | copy-done | bytes 4194328
  69.9 0.0 copy-start.2
  69.9 1.0 %copy-done.2 = bf16[512,1024]{1,0:T(8,128)(2,1)} copy-done((bf16[512,1024]{1,0:T(8,128)(2,1)}, bf16[512,1024]{1,0:T(8,128)(2,1)S(1)}, u32[]{:S(2)}) %copy-start.2) | copy-done | bytes 1048600
  70.9 0.0 copy-start.3
  70.9 0.6 copy-done.3
  71.5 0.0 copy-start.4
  71.5 0.6 copy-done.4
  72.1 0.0 copy-start.5
  72.1 0.6 copy-done.5
  72.7 4.9 %finish.1 = (bf16[512,4096]{1,0:T(8,128)(2,1)}, bf16[512,1024]{1,0:T(8,128)(2,1)}, f32[8,1024]{1,0:T(8,128)}, f32[8,1024]{1,0:T(8,128)}, f32[16,1024]{1,0:T(8,128)}) custom-call(bf16[512,4096]{1,0:T(8,128)(2,1)} %copy-done, bf16[512,1024]{1,0:T(8,128)(2,1)} %copy-done.2, f32[8,1024]{1,0:T(8,128)} %copy-done.4, f32[8,1024]{1,0:T(8,128)} %copy-done.5, ...), custom_call_target="tpu_custom_call" | custom-call | tf_op jit(solution)/shard_map/finish/pallas_call | solution.py:577
Async XLA Ops:
  0.6 1.2 %copy-start.1 = (bf16[1,512,1024]{2,1,0:T(8,128)(2,1)S(1)}, bf16[1,512,1024]{2,1,0:T(8,128)(2,1)}, u32[]{:S(2)}) copy-start(bf16[1,512,1024]{2,1,0:T(8,128)(2,1)} %param.8) | copy-start | bytes 3145732
  1.9 0.7 copy-start.6
  2.6 0.7 copy-start.7
  3.3 0.7 copy-start.8
  4.0 0.7 copy-start.9
  4.7 0.7 copy-start.10
  68.0 2.0 %copy-start = (bf16[512,4096]{1,0:T(8,128)(2,1)}, bf16[512,4096]{1,0:T(8,128)(2,1)S(1)}, u32[]{:S(2)}) copy-start(bf16[512,4096]{1,0:T(8,128)(2,1)S(1)} %get-tuple-element.15.refs_0_) | copy-start | bytes 12582916
  69.9 1.0 %copy-start.2 = (bf16[512,1024]{1,0:T(8,128)(2,1)}, bf16[512,1024]{1,0:T(8,128)(2,1)S(1)}, u32[]{:S(2)}) copy-start(bf16[512,1024]{1,0:T(8,128)(2,1)S(1)} %get-tuple-element.16.refs_1_) | copy-start | bytes 3145732
  70.9 0.6 copy-start.3
  71.5 0.6 copy-start.4
  72.1 0.6 copy-start.5

commit v3 on v2

--- a/solution.py
+++ b/solution.py
@@ -44,18 +44,23 @@
 def kernel(
     factor,
     query_hbm,
-    key_ref,
-    value_ref,
+    key_hbm,
+    value_hbm,
     weight_hbm,
     grad_hbm,
-    time_ref,
-    window_ref,
-    freq_ref,
+    time_hbm,
+    window_hbm,
+    freq_hbm,
     out_stage,
     qgrad,
     kgrad_ref,
     vgrad_ref,
     wgrad_ref,
+    key_ref,
+    value_ref,
+    time_ref,
+    window_ref,
+    freq_ref,
     q_raw,
     q_rot,
     near_kv,
@@ -107,6 +112,7 @@
     y_peer = [device(x, flip(y, m, 2), z, core) for m in (1, 2, 3)]
     z_peer = [device(x, y, flip(z, m, 3), core) for m in range(1, 8)]
     z_step = {d: device(x, y, (z + d + 8) % 8, core) for d in (1, -1, 2, -2)}
+    y_step = {d: device(x, (y + d + 4) % 4, z, core) for d in (1, -1)}
 
     counter = [0]
 
@@ -139,6 +145,13 @@
     pair_block = xh * 2 + 1 - core
     far_block = (1 - xh) * 2 + core
     far_pair_block = (1 - xh) * 2 + 1 - core
+    small = [
+        local(freq_hbm, freq_ref),
+        local(time_hbm, time_ref),
+        local(window_hbm, window_ref),
+        local(key_hbm, key_ref),
+        local(value_hbm, value_ref),
+    ]
     load_q = [local(query_hbm.at[:, pl.ds(i * GW, GW)], q_raw.at[i]) for i in range(GROUPS)]
     load_g = [local(grad_hbm.at[:, pl.ds(i * WIDTH, WIDTH)], g_own.at[i]) for i in range(4)]
     load_w = local(weight_hbm, w_all.at[block])
@@ -147,6 +160,9 @@
     greet = [pair, after, before] + x_peer + y_peer + z_peer
     for target in greet:
         pl.semaphore_signal(barrier, inc=1, device_id=target, device_id_type=MESH)
+
+    for copy in small:
+        copy.wait()
 
     lane_i = lax.broadcasted_iota(jnp.int32, (GW, GW), 0)
     lane_j = lax.broadcasted_iota(jnp.int32, (GW, GW), 1)
@@ -187,7 +203,7 @@
 
     halo_a = remote(near_kv.at[0], near_kv.at[1], after)
     halo_b = remote(near_kv.at[0], near_kv.at[2], before)
-    quarter = z % 4
+    quarter = (z + 2 * (y % 2)) % 4
     cross = []
     for half in range(2):
         rows = pl.ds(quarter * 256 + half * 128, 128)
@@ -263,15 +279,30 @@
 
     def pass_on(half):
         cross[half].wait_recv()
-        rows = pl.ds(quarter * 256 + half * 128, 128)
-        piece = w_all.at[far_block, rows]
+        start = quarter * 256 + half * 128
+        piece = w_all.at[far_block, pl.ds(start, 128)]
+        one = w_all.at[far_block, pl.ds(start, 64)]
+        two = w_all.at[far_block, pl.ds(start + 64, 64)]
+        up, down = (y_step[1], y_step[-1]) if half == 0 else (z_step[2], z_step[-2])
         moves = [
             remote(piece, piece, z_step[1]),
             remote(piece, piece, z_step[-1]),
-            remote(piece, piece, z_step[2 if half == 0 else -2]),
+            remote(one, one, up),
+            remote(two, two, down),
             remote(piece, piece, pair),
         ]
         far_moves.append(moves)
+
+    def hand_over(half):
+        for k, step in ((0, 3), (1, 1), (2, 2)):
+            far_moves[half][k].wait_recv()
+            if k == 2:
+                far_moves[half][3].wait_recv()
+            rows = pl.ds(((quarter + step) % 4) * 256 + half * 128, 128)
+            piece = w_all.at[far_block, rows]
+            far_moves[half].append(remote(piece, piece, pair))
+
+    pass_on(0)
 
     for copy in pair_g + pair_a:
         copy.wait_recv()
@@ -318,41 +349,18 @@
     send_x(1, 0)
     send_x(0, 0)
     send_x(1, 1)
-    pass_on(0)
+    gradient(0, 1, store_y(0))
+    for k in range(2):
+        send_y(k, 0, 0)
+    gradient(1, 1, store_y(1))
+    for k in range(2):
+        send_y(k, 0, 1)
     for h in range(2):
-        gradient(h, 1, store_y(h))
-        for slot in range(2):
-            for k in range(2):
-                send_y(k, slot, h)
+        for k in range(2):
+            send_y(k, 1, h)
+    pass_on(1)
     gradient(xh, 0, store_x(xh))
     send_x(0, 1)
-    pass_on(1)
-
-    x_second = []
-    y_second = []
-    for k in range(2):
-        to = flip(x, near[1 - k], 2)
-        x_first[k, 0].wait_recv()
-
-        @pl.loop(0, 4)
-        def _(i):
-            part = pl.ds(i * 2, 2)
-            s1[to, k, part] = (s1[to, k, part].astype(F32) + r1[k, 0, part].astype(F32)).astype(BF)
-
-        x_second.append(remote(s1.at[to, k], r1.at[k, 2], x_peer[near[1 - k] - 1]))
-    for k in range(2):
-        to = flip(y, near[1 - k], 2)
-        for h in range(2):
-            y_first[k, 0, h].wait_recv()
-
-            @pl.loop(0, 2)
-            def _(i):
-                part = pl.ds(i * 4, 4)
-                s2[to, k, h, part] = (
-                    s2[to, k, h, part].astype(F32) + r2[k, 0, h, part].astype(F32)
-                ).astype(BF)
-
-        y_second.append(remote(s2.at[to, k], r2.at[k, 2], y_peer[near[1 - k] - 1]))
 
     pair_w.wait_recv()
 
@@ -371,19 +379,37 @@
         rows = pl.ds(pl.multiple_of(j * 512, 512), 512)
         ag32[j] += dot(g_own[pair_block], w_all[pair_block, rows, :], NT)
 
+    x_second = []
+    y_second = []
+    for k in range(2):
+        to = flip(x, near[1 - k], 2)
+        x_first[k, 0].wait_recv()
+
+        @pl.loop(0, 4)
+        def _(i):
+            part = pl.ds(i * 2, 2)
+            s1[to, k, part] = (s1[to, k, part].astype(F32) + r1[k, 0, part].astype(F32)).astype(BF)
+
+        x_second.append(remote(s1.at[to, k], r1.at[k, 2], x_peer[near[1 - k] - 1]))
+
     project(block)
+
+    for k in range(2):
+        to = flip(y, near[1 - k], 2)
+        for h in range(2):
+            y_first[k, 0, h].wait_recv()
+
+            @pl.loop(0, 2)
+            def _(i):
+                part = pl.ds(i * 4, 4)
+                s2[to, k, h, part] = (
+                    s2[to, k, h, part].astype(F32) + r2[k, 0, h, part].astype(F32)
+                ).astype(BF)
+
+        y_second.append(remote(s2.at[to, k], r2.at[k, 2], y_peer[near[1 - k] - 1]))
+
     project(pair_block)
-
-    for half in range(2):
-        rows = [
-            pl.ds(((z + 3) % 4) * 256 + half * 128, 128),
-            pl.ds(((z + 1) % 4) * 256 + half * 128, 128),
-            pl.ds(((z + 2) % 4) * 256 + half * 128, 128),
-        ]
-        for k in range(3):
-            far_moves[half][k].wait_recv()
-            piece = w_all.at[far_block, rows[k]]
-            far_moves[half].append(remote(piece, piece, pair))
+    hand_over(0)
 
     for k in range(2):
         x_first[k, 1].wait_recv()
@@ -415,8 +441,9 @@
 
     x2_moves = [remote(t2.at[flip(x, m, 2)], p2.at[m - 1], x_peer[m - 1]) for m in (1, 2, 3)]
 
+    hand_over(1)
     for half in range(2):
-        for k in range(3, 7):
+        for k in range(4, 8):
             far_moves[half][k].wait_recv()
 
     @pl.loop(0, 2)
@@ -510,8 +537,8 @@
     factor = 1.0 / math.sqrt(TOK * lax.axis_size("ctx") * lax.axis_size("fsdp"))
 
     vmem = pl.BlockSpec(memory_space=pltpu.VMEM)
-    hbm = pl.BlockSpec(memory_space=pl.ANY)
-    n_sems = 56
+    hbm = pl.BlockSpec(memory_space=pltpu.HBM)
+    n_sems = 58
     results = [
         ((TOK, 4 * WIDTH), BF),
         ((TOK, WIDTH), BF),
@@ -520,6 +547,17 @@
         ((16, WIDTH), F32),
     ]
 
+    inputs = (
+        video_query[0],
+        audio_key[0],
+        audio_value[0],
+        out_weight,
+        grad_out[0],
+        query_time.reshape(1, TOK),
+        window,
+        jnp.asarray(freqs).reshape(1, 128),
+    )
+
     def body(*refs):
         kernel(factor, *refs)
 
@@ -527,9 +565,14 @@
         body,
         name="fused",
         out_shape=[pltpu.VMEM(shape, dtype) for shape, dtype in results],
-        in_specs=[hbm, vmem, vmem, hbm, hbm, vmem, vmem, vmem],
+        in_specs=[hbm] * 8,
         out_specs=[vmem] * 5,
         scratch_shapes=[
+            pltpu.VMEM((SPAN, WIDTH), BF),
+            pltpu.VMEM((SPAN, WIDTH), BF),
+            pltpu.VMEM((1, TOK), jnp.int32),
+            pltpu.VMEM((2, TOK), jnp.int32),
+            pltpu.VMEM((1, 128), F32),
             pltpu.VMEM((GROUPS, TOK, GW), BF),
             pltpu.VMEM((GROUPS, TOK, GW), BF),
             pltpu.VMEM((3, 2 * SPAN, WIDTH), BF),
@@ -565,14 +608,7 @@
             collective_id=0, has_side_effects=True, vmem_limit_bytes=46 << 20
         ),
     )(
-        video_query[0],
-        audio_key[0],
-        audio_value[0],
-        out_weight,
-        grad_out[0],
-        query_time.reshape(1, TOK),
-        window,
-        jnp.asarray(freqs).reshape(1, 128),
+        *[pltpu.with_memory_space_constraint(arg, pltpu.HBM) for arg in inputs]
     )
     outs = pl.pallas_call(
         finish,
@@ -581,7 +617,8 @@
         in_specs=[vmem] * 5,
         out_specs=[hbm] * 5,
         scratch_shapes=[pltpu.SemaphoreType.DMA((5,))],
-    )(*outs)
+        compiler_params=pltpu.CompilerParams(vmem_limit_bytes=4 << 20),
+    )(*[pltpu.with_memory_space_constraint(out, pltpu.VMEM) for out in outs])
     output, query_grad, key_grad, value_grad, weight_grad = outs
     return (output[None], query_grad[None], key_grad[None], value_grad[None], weight_grad)
 

time: 78.5 us -> 62.4 us (0.79)
  the two profiles are of different devices: /device:TPU:4 before, /device:TPU:1 now
where the time goes in v3:
time: 62.4 us; the launch traced here: 62.3 us
  Pallas kernels  61.7 us (99%)
  between operations  0.64 us (1%)
    pallas_call x1, Pallas kernels, local(): pl.pallas_call(body, name='fused', out_shape=[pltpu.VMEM(shape, dtype) fo...  59.3 us
    pallas_call x1, Pallas kernels, local(): pl.pallas_call(finish, name='finish', out_shape=[jax.ShapeDtypeStruct(sha...  2.4 us

profile of v3, /device:TPU:1, one launch (start us, length us, event | category | flops | bytes accessed | tf_op | source)
XLA Modules:
  0.0 62.3 jit_solution(128822733625046133)
XLA Ops:
  0.6 59.3 %fused.1 = (bf16[512,4096]{1,0:T(8,128)(2,1)S(1)}, bf16[512,1024]{1,0:T(8,128)(2,1)S(1)}, f32[8,1024]{1,0:T(8,128)S(1)}, f32[8,1024]{1,0:T(8,128)S(1)}, f32[16,1024]{1,0:T(8,128)S(1)}) custom-call(bf16[512,1024]{1,0:T(8,128)(2,1)} %bitcast.10, bf16[8,1024]{1,0:T(8,128)(2,1)} %bitcast.11, bf16[8,1024]{1,0:T(8,128)(2,1)} %bitcast.12, ...), custom_call_target="tpu_custom_call" | custom-call | tf_op jit(solution)/shard_map/fused/pallas_call | solution.py:564
  59.9 2.4 %finish.1 = (bf16[512,4096]{1,0:T(8,128)(2,1)}, bf16[512,1024]{1,0:T(8,128)(2,1)}, f32[8,1024]{1,0:T(8,128)}, f32[8,1024]{1,0:T(8,128)}, f32[16,1024]{1,0:T(8,128)}) custom-call(bf16[512,4096]{1,0:T(8,128)(2,1)S(1)} %get-tuple-element.15.refs_0_, bf16[512,1024]{1,0:T(8,128)(2,1)S(1)} %get-tuple-element.16.refs_1_, f32[8,1024]{1,0:T(8,128)S(1)} %get-tuple-element.17.refs_2_, ...), custom_call_target="tpu_custom_call" | custom-call | tf_op jit(solution)/shard_map/finish/pallas_call | solution.py:613

commit v4 on v3

--- a/solution.py
+++ b/solution.py
@@ -67,6 +67,8 @@
     w_all,
     g_own,
     g_pair,
+    keys_s,
+    values_s,
     probs_s,
     att,
     att_t,
@@ -114,6 +116,11 @@
     z_step = {d: device(x, y, (z + d + 8) % 8, core) for d in (1, -1, 2, -2)}
     y_step = {d: device(x, (y + d + 4) % 4, z, core) for d in (1, -1)}
 
+    barrier = pltpu.get_barrier_semaphore()
+    greet = [pair, after, before] + x_peer + y_peer + z_peer
+    for target in greet:
+        pl.semaphore_signal(barrier, inc=1, device_id=target, device_id_type=MESH)
+
     counter = [0]
 
     def remote(src, dst, target):
@@ -156,48 +163,24 @@
     load_g = [local(grad_hbm.at[:, pl.ds(i * WIDTH, WIDTH)], g_own.at[i]) for i in range(4)]
     load_w = local(weight_hbm, w_all.at[block])
 
-    barrier = pltpu.get_barrier_semaphore()
-    greet = [pair, after, before] + x_peer + y_peer + z_peer
-    for target in greet:
-        pl.semaphore_signal(barrier, inc=1, device_id=target, device_id_type=MESH)
-
     for copy in small:
         copy.wait()
 
-    lane_i = lax.broadcasted_iota(jnp.int32, (GW, GW), 0)
-    lane_j = lax.broadcasted_iota(jnp.int32, (GW, GW), 1)
-    first_j = lane_j % DH < HALF
-    turn = jnp.where(
-        first_j & (lane_i == lane_j + HALF),
-        -1.0,
-        jnp.where((~first_j) & (lane_i == lane_j - HALF), 1.0, 0.0),
+    lane = lax.broadcasted_iota(jnp.int32, (SPAN, WIDTH), 1) % DH
+
+    def turned(values):
+        left = pltpu.roll(values, WIDTH - HALF, 1)
+        right = pltpu.roll(values, HALF, 1)
+        return jnp.where(lane < HALF, -left, right)
+
+    own_row = lax.broadcasted_iota(jnp.int32, (SPAN, 1), 0) + ctx * SPAN
+    own_angles = own_row.astype(F32) * freq_ref[...]
+    cos_k = jnp.concatenate([jnp.cos(own_angles)] * (WIDTH // 128), axis=1)
+    sin_k = jnp.concatenate([jnp.sin(own_angles)] * (WIDTH // 128), axis=1)
+    raw_k = key_ref[...].astype(F32)
+    near_kv[0] = jnp.concatenate(
+        [raw_k * cos_k + turned(raw_k) * sin_k, value_ref[...].astype(F32)], axis=0
     ).astype(BF)
-    near_row = lax.broadcasted_iota(jnp.int32, (32, 1), 0) + ctx * SPAN - SPAN
-    angles = near_row.astype(F32) * freq_ref[...]
-    near_table = jnp.concatenate([jnp.cos(angles), jnp.sin(angles)], axis=1)
-    pieces = []
-    rest = near_table
-    for _ in range(3):
-        piece = rest.astype(BF).astype(F32)
-        pieces.append(piece)
-        rest = rest - piece
-    time_row = jnp.where(near_row == time_ref[...], 1.0, 0.0)
-    chosen = jnp.concatenate([time_row] * 3, axis=0).astype(BF)
-    table[...] = dot(chosen, jnp.concatenate(pieces, axis=0).astype(BF), TN)
-
-    def cos_q():
-        return jnp.concatenate([table[:, :128]] * 2, axis=1)
-
-    def sin_q():
-        return jnp.concatenate([table[:, 128:]] * 2, axis=1)
-
-    cos_k = jnp.concatenate([near_table[SPAN : 2 * SPAN, :128]] * 2, axis=1)
-    sin_k = jnp.concatenate([near_table[SPAN : 2 * SPAN, 128:]] * 2, axis=1)
-    for i in range(GROUPS):
-        sl = slice(i * GW, (i + 1) * GW)
-        raw = key_ref[:, sl]
-        turned = raw.astype(F32) * cos_k + dot(raw, turn, NN) * sin_k
-        near_kv[0, :, sl] = jnp.concatenate([turned, value_ref[:, sl].astype(F32)], axis=0).astype(BF)
 
     pl.semaphore_wait(barrier, len(greet))
 
@@ -217,6 +200,33 @@
         for h in range(2)
     ]
 
+    near_row = lax.broadcasted_iota(jnp.int32, (32, 1), 0) + ctx * SPAN - SPAN
+    angles = near_row.astype(F32) * freq_ref[...]
+    near_table = jnp.concatenate([jnp.cos(angles), jnp.sin(angles)], axis=1)
+    pieces = []
+    rest = near_table
+    for _ in range(3):
+        piece = rest.astype(BF).astype(F32)
+        pieces.append(piece)
+        rest = rest - piece
+    time_row = jnp.where(near_row == time_ref[...], 1.0, 0.0)
+    chosen = jnp.concatenate([time_row] * 3, axis=0).astype(BF)
+    table[...] = dot(chosen, jnp.concatenate(pieces, axis=0).astype(BF), TN)
+
+    def cos_q():
+        return jnp.concatenate([table[:, :128]] * 2, axis=1)
+
+    def sin_q():
+        return jnp.concatenate([table[:, 128:]] * 2, axis=1)
+
+    lane_i = lax.broadcasted_iota(jnp.int32, (GW, GW), 0)
+    lane_j = lax.broadcasted_iota(jnp.int32, (GW, GW), 1)
+    first_j = lane_j % DH < HALF
+    turn = jnp.where(
+        first_j & (lane_i == lane_j + HALF),
+        -1.0,
+        jnp.where((~first_j) & (lane_i == lane_j - HALF), 1.0, 0.0),
+    ).astype(BF)
     for copy in load_q:
         copy.wait()
 
@@ -260,6 +270,8 @@
     for i in range(GROUPS):
         keys = spread(0, i)
         values = spread(SPAN, i)
+        keys_s[i] = keys
+        values_s[i] = values
         scores = SCALE * dot(keys, q_rot[i], NT).reshape(GH, NEAR, TOK)
         masked = jnp.where(allowed[None], scores, -1e30)
         highest = jnp.max(masked, axis=1, keepdims=True)
@@ -270,7 +282,6 @@
         rows = pl.ds(i * GW, GW)
         att_t[rows, :] = dot(values, low, TN).astype(BF)
         pair_a.append(remote(att_t.at[rows], att_t_pair.at[rows], pair))
-        att[i] = dot(low, values, TN).astype(BF)
 
     pair_w = remote(weight_hbm, w_all.at[block], pair)
     early(1)
@@ -304,65 +315,95 @@
 
     pass_on(0)
 
-    for copy in pair_g + pair_a:
+    for copy in pair_g + pair_a[:2]:
         copy.wait_recv()
 
-    def gradient(h, part, store):
+    def gradient(h, part, i, store):
         cols = slice(part * 512, (part + 1) * 512)
-
-        @pl.loop(0, 2)
-        def _(i):
-            rows = pl.ds(pl.multiple_of(i * 512, 512), 512)
-            total = dot(att_t[rows, :], g_own[2 * h + core, :, cols], NN)
-            total = total + dot(att_t_pair[rows, :], g_pair[h, :, cols], NN)
-            store(i, total.astype(BF).reshape(4, 4, 2, 16, 512))
-
-    def store_x(h):
-        def store(i, total):
-            for low_x in range(2):
-                for k in range(2):
-                    s1[2 * h + low_x, k, pl.ds(i * 4, 4)] = total[:, :, low_x, :, k * 256 : k * 256 + 256]
-
-        return store
-
-    def store_y(h):
-        def store(i, total):
-            for to_y in range(4):
-                for k in range(2):
-                    s2[to_y, k, h, pl.ds(i * 4, 4)] = total[:, to_y, :, :, k * 256 : k * 256 + 256]
-
-        return store
+        rows = slice(i * 512, (i + 1) * 512)
+        total = dot(att_t[rows, :], g_own[2 * h + core, :, cols], NN)
+        total = total + dot(att_t_pair[rows, :], g_pair[h, :, cols], NN)
+        store(h, i, total.astype(BF).reshape(4, 4, 2, 16, 512))
+
+    def store_x(h, i, total):
+        for low_x in range(2):
+            for k in range(2):
+                s1[2 * h + low_x, k, i] = total[:, :, low_x, :, k * 256 : k * 256 + 256]
+
+    def store_y(h, i, total):
+        for to_y in range(4):
+            for k in range(2):
+                s2[to_y, k, i, h] = total[:, to_y, :, :, k * 256 : k * 256 + 256]
 
     near = (1, 3)
     x_first = {}
     y_first = {}
 
-    def send_x(k, slot):
+    def send_x(k, slot, i):
         to = flip(x, 2 if slot == 0 else near[k], 2)
-        x_first[k, slot] = remote(s1.at[to, k], r1.at[k, slot], x_peer[near[k] - 1])
-
-    def send_y(k, slot, h):
+        x_first[k, slot, i] = remote(s1.at[to, k, i], r1.at[k, slot, i], x_peer[near[k] - 1])
+
+    def send_y(k, slot, i, h=None):
         to = flip(y, 2 if slot == 0 else near[k], 2)
-        y_first[k, slot, h] = remote(s2.at[to, k, h], r2.at[k, slot, h], y_peer[near[k] - 1])
-
-    gradient(1 - xh, 0, store_x(1 - xh))
-    send_x(1, 0)
-    send_x(0, 0)
-    send_x(1, 1)
-    gradient(0, 1, store_y(0))
-    for k in range(2):
-        send_y(k, 0, 0)
-    gradient(1, 1, store_y(1))
-    for k in range(2):
-        send_y(k, 0, 1)
-    for h in range(2):
+        piece = s2.at[to, k, i] if h is None else s2.at[to, k, i, h]
+        place = r2.at[k, slot, i] if h is None else r2.at[k, slot, i, h]
+        y_first.setdefault((k, slot, i), []).append(remote(piece, place, y_peer[near[k] - 1]))
+
+    x_second = {}
+    y_second = {}
+
+    def pass_x(i):
         for k in range(2):
-            send_y(k, 1, h)
+            to = flip(x, near[1 - k], 2)
+            x_first[k, 0, i].wait_recv()
+            s1[to, k, i] = (s1[to, k, i].astype(F32) + r1[k, 0, i].astype(F32)).astype(BF)
+            x_second[k, i] = remote(s1.at[to, k, i], r1.at[k, 2, i], x_peer[near[1 - k] - 1])
+
+    def pass_y(i):
+        for k in range(2):
+            to = flip(y, near[1 - k], 2)
+            for copy in y_first[k, 0, i]:
+                copy.wait_recv()
+            s2[to, k, i] = (s2[to, k, i].astype(F32) + r2[k, 0, i].astype(F32)).astype(BF)
+            y_second[k, i] = remote(s2.at[to, k, i], r2.at[k, 2, i], y_peer[near[1 - k] - 1])
+
+    gradient(1 - xh, 0, 0, store_x)
+    send_x(1, 0, 0)
+    send_x(0, 0, 0)
+    send_x(1, 1, 0)
+    gradient(0, 1, 0, store_y)
+    send_y(0, 0, 0, 0)
+    send_y(1, 0, 0, 0)
+    gradient(1, 1, 0, store_y)
+    send_y(0, 0, 0, 1)
+    send_y(1, 0, 0, 1)
+    send_y(0, 1, 0)
+    send_y(1, 1, 0)
+    gradient(xh, 0, 0, store_x)
+    send_x(0, 1, 0)
+    for copy in pair_a[2:]:
+        copy.wait_recv()
+    gradient(1 - xh, 0, 1, store_x)
+    send_x(1, 0, 1)
+    send_x(0, 0, 1)
     pass_on(1)
-    gradient(xh, 0, store_x(xh))
-    send_x(0, 1)
+    pass_x(0)
+    send_x(1, 1, 1)
+    gradient(0, 1, 1, store_y)
+    gradient(1, 1, 1, store_y)
+    send_y(0, 0, 1)
+    send_y(1, 0, 1)
+    pass_y(0)
+    send_y(0, 1, 1)
+    send_y(1, 1, 1)
+    gradient(xh, 0, 1, store_x)
+    send_x(0, 1, 1)
 
     pair_w.wait_recv()
+
+    @pl.loop(0, GROUPS)
+    def _(i):
+        att[i] = dot(probs_s[i].astype(BF), values_s[i], TN).astype(BF)
 
     def project(b):
         @pl.loop(0, 2)
@@ -379,69 +420,84 @@
         rows = pl.ds(pl.multiple_of(j * 512, 512), 512)
         ag32[j] += dot(g_own[pair_block], w_all[pair_block, rows, :], NT)
 
-    x_second = []
-    y_second = []
-    for k in range(2):
-        to = flip(x, near[1 - k], 2)
-        x_first[k, 0].wait_recv()
-
-        @pl.loop(0, 4)
-        def _(i):
-            part = pl.ds(i * 2, 2)
-            s1[to, k, part] = (s1[to, k, part].astype(F32) + r1[k, 0, part].astype(F32)).astype(BF)
-
-        x_second.append(remote(s1.at[to, k], r1.at[k, 2], x_peer[near[1 - k] - 1]))
-
     project(block)
-
-    for k in range(2):
-        to = flip(y, near[1 - k], 2)
-        for h in range(2):
-            y_first[k, 0, h].wait_recv()
-
-            @pl.loop(0, 2)
-            def _(i):
-                part = pl.ds(i * 4, 4)
-                s2[to, k, h, part] = (
-                    s2[to, k, h, part].astype(F32) + r2[k, 0, h, part].astype(F32)
-                ).astype(BF)
-
-        y_second.append(remote(s2.at[to, k], r2.at[k, 2], y_peer[near[1 - k] - 1]))
-
+    pass_x(1)
+    pass_y(1)
+
+    y2_moves = {}
+    x2_moves = {}
+
+    def second_y(i):
+        for k in range(2):
+            x_first[k, 1, i].wait_recv()
+            x_second[k, i].wait_recv()
+        y2_moves[i] = []
+        for m in (2, 1, 3, 0):
+            to = flip(y, m, 2)
+            for k in range(2):
+                total = s1[x, k, i, :, to].astype(F32)
+                for j in (1, 2):
+                    total = total + r1[k, j, i, :, to].astype(F32)
+                t1[i, to, :, :, k * 256 : k * 256 + 256] = total.astype(BF)
+            if m:
+                y2_moves[i].append(remote(t1.at[i, to], p1.at[i, m - 1], y_peer[m - 1]))
+
+    def second_x(i):
+        for k in range(2):
+            for copy in y_first[k, 1, i]:
+                copy.wait_recv()
+            y_second[k, i].wait_recv()
+        x2_moves[i] = []
+        for m in (2, 1, 3, 0):
+            to = flip(x, m, 2)
+            h = flip(xh, m // 2, 1)
+            low_x = flip(xl, m % 2, 1)
+            for k in range(2):
+                total = s2[y, k, i, h, :, low_x].astype(F32)
+                for j in (1, 2):
+                    total = total + r2[k, j, i, h, :, low_x].astype(F32)
+                t2[i, to, :, :, k * 256 : k * 256 + 256] = total.astype(BF)
+            if m:
+                x2_moves[i].append(remote(t2.at[i, to], p2.at[i, m - 1], x_peer[m - 1]))
+
+    z_base = counter[0]
+    counter[0] += 14
+
+    def z_move(part, m):
+        index = z_base + part * 7 + m - 1
+        return pltpu.make_async_remote_copy(
+            src_ref=u.at[part, flip(z, m, 3)],
+            dst_ref=v.at[part, m - 1],
+            send_sem=sem_s.at[index],
+            recv_sem=sem_r.at[index],
+            device_id=z_peer[m - 1],
+            device_id_type=MESH,
+        )
+
+    def third(part, i):
+        moves, mine, pieces = (y2_moves[i], t1[i, y], p1) if part == 0 else (x2_moves[i], t2[i, x], p2)
+        for copy in moves:
+            copy.wait_recv()
+        total = mine.astype(F32)
+        for m in range(3):
+            total = total + pieces[i, m].astype(F32)
+        u[part, 4 * i : 4 * i + 4] = total.astype(BF)
+        for m in (4, 3, 5, 2, 6, 1, 7):
+
+            @pl.when(flip(z, m, 3) // 4 == i)
+            def _():
+                z_move(part, m).start()
+
+    second_y(0)
+    second_x(0)
     project(pair_block)
     hand_over(0)
-
-    for k in range(2):
-        x_first[k, 1].wait_recv()
-        x_second[k].wait_recv()
-
-    @pl.loop(0, 4)
-    def _(to_y):
-        for k in range(2):
-            total = s1[x, k, :, to_y].astype(F32)
-            for m in (1, 2):
-                total = total + r1[k, m, :, to_y].astype(F32)
-            t1[to_y, :, :, k * 256 : k * 256 + 256] = total.astype(BF)
-
-    y2_moves = [remote(t1.at[flip(y, m, 2)], p1.at[m - 1], y_peer[m - 1]) for m in (1, 2, 3)]
-    for k in range(2):
-        for h in range(2):
-            y_first[k, 1, h].wait_recv()
-        y_second[k].wait_recv()
-
-    @pl.loop(0, 4)
-    def _(to_x):
-        h = to_x // 2
-        low_x = to_x % 2
-        for k in range(2):
-            total = s2[y, k, h, :, low_x].astype(F32)
-            for m in (1, 2):
-                total = total + r2[k, m, h, :, low_x].astype(F32)
-            t2[to_x, :, :, k * 256 : k * 256 + 256] = total.astype(BF)
-
-    x2_moves = [remote(t2.at[flip(x, m, 2)], p2.at[m - 1], x_peer[m - 1]) for m in (1, 2, 3)]
-
     hand_over(1)
+    third(0, 0)
+    second_y(1)
+    third(1, 0)
+    second_x(1)
+
     for half in range(2):
         for k in range(4, 8):
             far_moves[half][k].wait_recv()
@@ -455,10 +511,13 @@
         ag[2 * j] = low[:, :GW]
         ag[2 * j + 1] = low[:, GW:]
 
+    third(0, 1)
+    third(1, 1)
+
     @pl.loop(0, GROUPS)
     def _(i):
-        keys = spread(0, i)
-        values = spread(SPAN, i)
+        keys = keys_s[i]
+        values = values_s[i]
         grads = ag[i]
         probs = probs_s[i]
         low = probs.astype(BF)
@@ -484,43 +543,28 @@
     ]
 
     project(far_block)
-
-    for copy in y2_moves + x2_moves:
-        copy.wait_recv()
-    first = t1[y].astype(F32)
-    second = t2[x].astype(F32)
-    for m in range(3):
-        first = first + p1[m].astype(F32)
-        second = second + p2[m].astype(F32)
-    u[:, :, 0:512] = first.astype(BF)
-    u[:, :, 512:1024] = second.astype(BF)
-    z_moves = [remote(u.at[flip(z, m, 3)], v.at[m - 1], z_peer[m - 1]) for m in range(1, 8)]
-
     project(far_pair_block)
 
     for copy in back:
         copy.wait_recv()
     vgrad_ref[...] = vp[SPAN : 2 * SPAN, :] + halo_in[0, SPAN:] + halo_in[1, SPAN:]
     key_total = kp[SPAN : 2 * SPAN, :] + halo_in[0, 0:SPAN] + halo_in[1, 0:SPAN]
-    lane = lax.broadcasted_iota(jnp.int32, (SPAN, WIDTH), 1) % DH
-    other = jnp.where(
-        lane < HALF,
-        -pltpu.roll(key_total, WIDTH - HALF, 1),
-        pltpu.roll(key_total, HALF, 1),
-    )
-    wide_cos = jnp.concatenate([cos_k] * GROUPS, axis=1)
-    wide_sin = jnp.concatenate([sin_k] * GROUPS, axis=1)
-    kgrad_ref[...] = key_total * wide_cos - other * wide_sin
-
-    for copy in z_moves:
-        copy.wait_recv()
-    total = u[z].astype(F32)
-    for m in range(7):
-        total = total + v[m].astype(F32)
-    wgrad_ref[...] = total * factor
+    kgrad_ref[...] = key_total * cos_k - turned(key_total) * sin_k
+
+    for part in range(2):
+        for m in range(1, 8):
+            z_move(part, m).wait_recv()
+    for part in range(2):
+        total = u[part, z].astype(F32)
+        for m in range(7):
+            total = total + v[part, m].astype(F32)
+        wgrad_ref[:, part * 512 : part * 512 + 512] = total * factor
 
     for copy in started:
         copy.wait_send()
+    for part in range(2):
+        for m in range(1, 8):
+            z_move(part, m).wait_send()
 
 
 def finish(*refs):
@@ -538,7 +582,7 @@
 
     vmem = pl.BlockSpec(memory_space=pltpu.VMEM)
     hbm = pl.BlockSpec(memory_space=pltpu.HBM)
-    n_sems = 58
+    n_sems = 88
     results = [
         ((TOK, 4 * WIDTH), BF),
         ((TOK, WIDTH), BF),
@@ -579,6 +623,8 @@
             pltpu.VMEM((4, WIDTH, WIDTH), BF),
             pltpu.VMEM((4, TOK, WIDTH), BF),
             pltpu.VMEM((2, TOK, WIDTH), BF),
+            pltpu.VMEM((GROUPS, GH * NEAR, GW), BF),
+            pltpu.VMEM((GROUPS, GH * NEAR, GW), BF),
             pltpu.VMEM((GROUPS, GH * NEAR, TOK), F32),
             pltpu.VMEM((GROUPS, TOK, GW), BF),
             pltpu.VMEM((WIDTH, TOK), BF),
@@ -590,16 +636,16 @@
             pltpu.VMEM((NEAR, WIDTH), F32),
             pltpu.VMEM((2, 2 * SPAN, WIDTH), F32),
             pltpu.VMEM((2, 2 * SPAN, WIDTH), F32),
-            pltpu.VMEM((4, 2, 8, 4, 16, 256), BF),
-            pltpu.VMEM((2, 3, 8, 4, 16, 256), BF),
-            pltpu.VMEM((4, 2, 2, 8, 2, 16, 256), BF),
-            pltpu.VMEM((2, 3, 2, 8, 2, 16, 256), BF),
-            pltpu.VMEM((4, 8, 16, 512), BF),
-            pltpu.VMEM((3, 8, 16, 512), BF),
-            pltpu.VMEM((4, 8, 16, 512), BF),
-            pltpu.VMEM((3, 8, 16, 512), BF),
-            pltpu.VMEM((8, 16, WIDTH), BF),
-            pltpu.VMEM((7, 16, WIDTH), BF),
+            pltpu.VMEM((4, 2, 2, 4, 4, 16, 256), BF),
+            pltpu.VMEM((2, 3, 2, 4, 4, 16, 256), BF),
+            pltpu.VMEM((4, 2, 2, 2, 4, 2, 16, 256), BF),
+            pltpu.VMEM((2, 3, 2, 2, 4, 2, 16, 256), BF),
+            pltpu.VMEM((2, 4, 4, 16, 512), BF),
+            pltpu.VMEM((2, 3, 4, 16, 512), BF),
+            pltpu.VMEM((2, 4, 4, 16, 512), BF),
+            pltpu.VMEM((2, 3, 4, 16, 512), BF),
+            pltpu.VMEM((2, 8, 16, 512), BF),
+            pltpu.VMEM((2, 7, 16, 512), BF),
             pltpu.SemaphoreType.DMA((24,)),
             pltpu.SemaphoreType.DMA((n_sems,)),
             pltpu.SemaphoreType.DMA((n_sems,)),

time: 62.4 us -> 60.2 us (0.965)
  the two profiles are of different devices: /device:TPU:1 before, /device:TPU:4 now
where the time goes in v4:
time: 60.2 us; the launch traced here: 60.1 us
  Pallas kernels  59.4 us (99%)
  between operations  0.64 us (1%)
    pallas_call x1, Pallas kernels, local(): pl.pallas_call(body, name='fused', out_shape=[pltpu.VMEM(shape, dtype) fo...  57 us
    pallas_call x1, Pallas kernels, local(): pl.pallas_call(finish, name='finish', out_shape=[jax.ShapeDtypeStruct(sha...  2.4 us

profile of v4, /device:TPU:4, one launch (start us, length us, event | category | flops | bytes accessed | tf_op | source)
XLA Modules:
  0.0 60.1 jit_solution(14767199756903562962)
XLA Ops:
  0.6 57.0 %fused.1 = (bf16[512,4096]{1,0:T(8,128)(2,1)S(1)}, bf16[512,1024]{1,0:T(8,128)(2,1)S(1)}, f32[8,1024]{1,0:T(8,128)S(1)}, f32[8,1024]{1,0:T(8,128)S(1)}, f32[16,1024]{1,0:T(8,128)S(1)}) custom-call(bf16[512,1024]{1,0:T(8,128)(2,1)} %bitcast.10, bf16[8,1024]{1,0:T(8,128)(2,1)} %bitcast.11, bf16[8,1024]{1,0:T(8,128)(2,1)} %bitcast.12, ...), custom_call_target="tpu_custom_call" | custom-call | tf_op jit(solution)/shard_map/fused/pallas_call | solution.py:608
  57.7 2.4 %finish.1 = (bf16[512,4096]{1,0:T(8,128)(2,1)}, bf16[512,1024]{1,0:T(8,128)(2,1)}, f32[8,1024]{1,0:T(8,128)}, f32[8,1024]{1,0:T(8,128)}, f32[16,1024]{1,0:T(8,128)}) custom-call(bf16[512,4096]{1,0:T(8,128)(2,1)S(1)} %get-tuple-element.15.refs_0_, bf16[512,1024]{1,0:T(8,128)(2,1)S(1)} %get-tuple-element.16.refs_1_, f32[8,1024]{1,0:T(8,128)S(1)} %get-tuple-element.17.refs_2_, ...), custom_call_target="tpu_custom_call" | custom-call | tf_op jit(solution)/shard_map/finish/pallas_call | solution.py:659

commit v5 on v4

--- a/solution.py
+++ b/solution.py
@@ -17,6 +17,7 @@
 GROUPS = 4
 GW = WIDTH // GROUPS
 GH = GW // DH
+WIDE = 384
 SCALE = 1.0 / math.sqrt(DH)
 MESH = pl.DeviceIdType.MESH
 BF = jnp.bfloat16
@@ -50,7 +51,6 @@
     grad_hbm,
     time_hbm,
     window_hbm,
-    freq_hbm,
     out_stage,
     qgrad,
     kgrad_ref,
@@ -60,7 +60,6 @@
     value_ref,
     time_ref,
     window_ref,
-    freq_ref,
     q_raw,
     q_rot,
     near_kv,
@@ -80,8 +79,10 @@
     vp,
     halo_out,
     halo_in,
-    s1,
-    r1,
+    s1a,
+    s1b,
+    r1a,
+    r1b,
     s2,
     r2,
     t1,
@@ -116,11 +117,6 @@
     z_step = {d: device(x, y, (z + d + 8) % 8, core) for d in (1, -1, 2, -2)}
     y_step = {d: device(x, (y + d + 4) % 4, z, core) for d in (1, -1)}
 
-    barrier = pltpu.get_barrier_semaphore()
-    greet = [pair, after, before] + x_peer + y_peer + z_peer
-    for target in greet:
-        pl.semaphore_signal(barrier, inc=1, device_id=target, device_id_type=MESH)
-
     counter = [0]
 
     def remote(src, dst, target):
@@ -153,18 +149,20 @@
     far_block = (1 - xh) * 2 + core
     far_pair_block = (1 - xh) * 2 + 1 - core
     small = [
-        local(freq_hbm, freq_ref),
+        local(key_hbm, key_ref),
+        local(value_hbm, value_ref),
         local(time_hbm, time_ref),
         local(window_hbm, window_ref),
-        local(key_hbm, key_ref),
-        local(value_hbm, value_ref),
     ]
+
+    barrier = pltpu.get_barrier_semaphore()
+    greet = [pair, after, before] + x_peer + y_peer + z_peer
+    for target in greet:
+        pl.semaphore_signal(barrier, inc=1, device_id=target, device_id_type=MESH)
+
     load_q = [local(query_hbm.at[:, pl.ds(i * GW, GW)], q_raw.at[i]) for i in range(GROUPS)]
     load_g = [local(grad_hbm.at[:, pl.ds(i * WIDTH, WIDTH)], g_own.at[i]) for i in range(4)]
     load_w = local(weight_hbm, w_all.at[block])
-
-    for copy in small:
-        copy.wait()
 
     lane = lax.broadcasted_iota(jnp.int32, (SPAN, WIDTH), 1) % DH
 
@@ -173,10 +171,16 @@
         right = pltpu.roll(values, HALF, 1)
         return jnp.where(lane < HALF, -left, right)
 
+    freqs = jnp.zeros((1, 128), F32)
+    frequency = lax.broadcasted_iota(jnp.int32, (1, 128), 1) % HALF
+    for m in range(HALF):
+        freqs = jnp.where(frequency == m, np.float32(10000.0 ** (-m / HALF)), freqs)
     own_row = lax.broadcasted_iota(jnp.int32, (SPAN, 1), 0) + ctx * SPAN
-    own_angles = own_row.astype(F32) * freq_ref[...]
+    own_angles = own_row.astype(F32) * freqs
     cos_k = jnp.concatenate([jnp.cos(own_angles)] * (WIDTH // 128), axis=1)
     sin_k = jnp.concatenate([jnp.sin(own_angles)] * (WIDTH // 128), axis=1)
+    for copy in small:
+        copy.wait()
     raw_k = key_ref[...].astype(F32)
     near_kv[0] = jnp.concatenate(
         [raw_k * cos_k + turned(raw_k) * sin_k, value_ref[...].astype(F32)], axis=0
@@ -201,7 +205,7 @@
     ]
 
     near_row = lax.broadcasted_iota(jnp.int32, (32, 1), 0) + ctx * SPAN - SPAN
-    angles = near_row.astype(F32) * freq_ref[...]
+    angles = near_row.astype(F32) * freqs
     near_table = jnp.concatenate([jnp.cos(angles), jnp.sin(angles)], axis=1)
     pieces = []
     rest = near_table
@@ -325,10 +329,13 @@
         total = total + dot(att_t_pair[rows, :], g_pair[h, :, cols], NN)
         store(h, i, total.astype(BF).reshape(4, 4, 2, 16, 512))
 
+    s1, r1 = (s1a, s1b), (r1a, r1b)
+    x_cols = (slice(0, WIDE), slice(WIDE, 512))
+
     def store_x(h, i, total):
         for low_x in range(2):
             for k in range(2):
-                s1[2 * h + low_x, k, i] = total[:, :, low_x, :, k * 256 : k * 256 + 256]
+                s1[k][2 * h + low_x, i] = total[:, :, low_x, :, x_cols[k]]
 
     def store_y(h, i, total):
         for to_y in range(4):
@@ -341,7 +348,7 @@
 
     def send_x(k, slot, i):
         to = flip(x, 2 if slot == 0 else near[k], 2)
-        x_first[k, slot, i] = remote(s1.at[to, k, i], r1.at[k, slot, i], x_peer[near[k] - 1])
+        x_first[k, slot, i] = remote(s1[k].at[to, i], r1[k].at[slot, i], x_peer[near[k] - 1])
 
     def send_y(k, slot, i, h=None):
         to = flip(y, 2 if slot == 0 else near[k], 2)
@@ -356,8 +363,8 @@
         for k in range(2):
             to = flip(x, near[1 - k], 2)
             x_first[k, 0, i].wait_recv()
-            s1[to, k, i] = (s1[to, k, i].astype(F32) + r1[k, 0, i].astype(F32)).astype(BF)
-            x_second[k, i] = remote(s1.at[to, k, i], r1.at[k, 2, i], x_peer[near[1 - k] - 1])
+            s1[k][to, i] = (s1[k][to, i].astype(F32) + r1[k][0, i].astype(F32)).astype(BF)
+            x_second[k, i] = remote(s1[k].at[to, i], r1[k].at[2, i], x_peer[near[1 - k] - 1])
 
     def pass_y(i):
         for k in range(2):
@@ -367,13 +374,13 @@
             s2[to, k, i] = (s2[to, k, i].astype(F32) + r2[k, 0, i].astype(F32)).astype(BF)
             y_second[k, i] = remote(s2.at[to, k, i], r2.at[k, 2, i], y_peer[near[1 - k] - 1])
 
-    gradient(1 - xh, 0, 0, store_x)
-    send_x(1, 0, 0)
-    send_x(0, 0, 0)
-    send_x(1, 1, 0)
     gradient(0, 1, 0, store_y)
     send_y(0, 0, 0, 0)
     send_y(1, 0, 0, 0)
+    gradient(1 - xh, 0, 0, store_x)
+    send_x(0, 0, 0)
+    send_x(1, 0, 0)
+    send_x(1, 1, 0)
     gradient(1, 1, 0, store_y)
     send_y(0, 0, 0, 1)
     send_y(1, 0, 0, 1)
@@ -386,18 +393,18 @@
     gradient(1 - xh, 0, 1, store_x)
     send_x(1, 0, 1)
     send_x(0, 0, 1)
-    pass_on(1)
-    pass_x(0)
-    send_x(1, 1, 1)
     gradient(0, 1, 1, store_y)
     gradient(1, 1, 1, store_y)
     send_y(0, 0, 1)
     send_y(1, 0, 1)
+    pass_on(1)
+    gradient(xh, 0, 1, store_x)
+    pass_x(0)
+    send_x(1, 1, 1)
+    send_x(0, 1, 1)
     pass_y(0)
     send_y(0, 1, 1)
     send_y(1, 1, 1)
-    gradient(xh, 0, 1, store_x)
-    send_x(0, 1, 1)
 
     pair_w.wait_recv()
 
@@ -435,10 +442,10 @@
         for m in (2, 1, 3, 0):
             to = flip(y, m, 2)
             for k in range(2):
-                total = s1[x, k, i, :, to].astype(F32)
+                total = s1[k][x, i, :, to].astype(F32)
                 for j in (1, 2):
-                    total = total + r1[k, j, i, :, to].astype(F32)
-                t1[i, to, :, :, k * 256 : k * 256 + 256] = total.astype(BF)
+                    total = total + r1[k][j, i, :, to].astype(F32)
+                t1[i, to, :, :, x_cols[k]] = total.astype(BF)
             if m:
                 y2_moves[i].append(remote(t1.at[i, to], p1.at[i, m - 1], y_peer[m - 1]))
 
@@ -577,7 +584,6 @@
 
 
 def local(video_query, audio_key, audio_value, out_weight, grad_out, query_time, window):
-    freqs = np.tile((10000.0 ** (-np.arange(HALF) / HALF)).astype(np.float32), 128 // HALF)
     factor = 1.0 / math.sqrt(TOK * lax.axis_size("ctx") * lax.axis_size("fsdp"))
 
     vmem = pl.BlockSpec(memory_space=pltpu.VMEM)
@@ -599,7 +605,6 @@
         grad_out[0],
         query_time.reshape(1, TOK),
         window,
-        jnp.asarray(freqs).reshape(1, 128),
     )
 
     def body(*refs):
@@ -609,14 +614,13 @@
         body,
         name="fused",
         out_shape=[pltpu.VMEM(shape, dtype) for shape, dtype in results],
-        in_specs=[hbm] * 8,
+        in_specs=[hbm] * 7,
         out_specs=[vmem] * 5,
         scratch_shapes=[
             pltpu.VMEM((SPAN, WIDTH), BF),
             pltpu.VMEM((SPAN, WIDTH), BF),
             pltpu.VMEM((1, TOK), jnp.int32),
             pltpu.VMEM((2, TOK), jnp.int32),
-            pltpu.VMEM((1, 128), F32),
             pltpu.VMEM((GROUPS, TOK, GW), BF),
             pltpu.VMEM((GROUPS, TOK, GW), BF),
             pltpu.VMEM((3, 2 * SPAN, WIDTH), BF),
@@ -636,8 +640,10 @@
             pltpu.VMEM((NEAR, WIDTH), F32),
             pltpu.VMEM((2, 2 * SPAN, WIDTH), F32),
             pltpu.VMEM((2, 2 * SPAN, WIDTH), F32),
-            pltpu.VMEM((4, 2, 2, 4, 4, 16, 256), BF),
-            pltpu.VMEM((2, 3, 2, 4, 4, 16, 256), BF),
+            pltpu.VMEM((4, 2, 4, 4, 16, WIDE), BF),
+            pltpu.VMEM((4, 2, 4, 4, 16, 512 - WIDE), BF),
+            pltpu.VMEM((3, 2, 4, 4, 16, WIDE), BF),
+            pltpu.VMEM((3, 2, 4, 4, 16, 512 - WIDE), BF),
             pltpu.VMEM((4, 2, 2, 2, 4, 2, 16, 256), BF),
             pltpu.VMEM((2, 3, 2, 2, 4, 2, 16, 256), BF),
             pltpu.VMEM((2, 4, 4, 16, 512), BF),

time: 60.2 us -> 60 us (level)
  no operation moved by 1% of the time
where the time goes in v5:
time: 60 us; the launch traced here: 59.8 us
  Pallas kernels  59.1 us (98%)
  between operations  0.64 us (1%)
    pallas_call x1, Pallas kernels, local(): pl.pallas_call(body, name='fused', out_shape=[pltpu.VMEM(shape, dtype) fo...  56.7 us
    pallas_call x1, Pallas kernels, local(): pl.pallas_call(finish, name='finish', out_shape=[jax.ShapeDtypeStruct(sha...  2.4 us

profile of v5, /device:TPU:4, one launch (start us, length us, event | category | flops | bytes accessed | tf_op | source)
XLA Modules:
  0.0 59.8 jit_solution(16161210280717018708)
XLA Ops:
  0.6 56.7 %fused.1 = (bf16[512,4096]{1,0:T(8,128)(2,1)S(1)}, bf16[512,1024]{1,0:T(8,128)(2,1)S(1)}, f32[8,1024]{1,0:T(8,128)S(1)}, f32[8,1024]{1,0:T(8,128)S(1)}, f32[16,1024]{1,0:T(8,128)S(1)}) custom-call(bf16[512,1024]{1,0:T(8,128)(2,1)} %bitcast.10, bf16[8,1024]{1,0:T(8,128)(2,1)} %bitcast.11, bf16[8,1024]{1,0:T(8,128)(2,1)} %bitcast.12, ...), custom_call_target="tpu_custom_call" | custom-call | tf_op jit(solution)/shard_map/fused/pallas_call | solution.py:613
  57.4 2.4 %finish.1 = (bf16[512,4096]{1,0:T(8,128)(2,1)}, bf16[512,1024]{1,0:T(8,128)(2,1)}, f32[8,1024]{1,0:T(8,128)}, f32[8,1024]{1,0:T(8,128)}, f32[16,1024]{1,0:T(8,128)}) custom-call(bf16[512,4096]{1,0:T(8,128)(2,1)S(1)} %get-tuple-element.15.refs_0_, bf16[512,1024]{1,0:T(8,128)(2,1)S(1)} %get-tuple-element.16.refs_1_, f32[8,1024]{1,0:T(8,128)S(1)} %get-tuple-element.17.refs_2_, ...), custom_call_target="tpu_custom_call" | custom-call | tf_op jit(solution)/shard_map/finish/pallas_call | solution.py:665

commit v6 on v5

--- a/solution.py
+++ b/solution.py
@@ -45,8 +45,7 @@
 def kernel(
     factor,
     query_hbm,
-    key_hbm,
-    value_hbm,
+    pair_hbm,
     weight_hbm,
     grad_hbm,
     time_hbm,
@@ -56,8 +55,7 @@
     kgrad_ref,
     vgrad_ref,
     wgrad_ref,
-    key_ref,
-    value_ref,
+    pair_ref,
     time_ref,
     window_ref,
     q_raw,
@@ -149,8 +147,7 @@
     far_block = (1 - xh) * 2 + core
     far_pair_block = (1 - xh) * 2 + 1 - core
     small = [
-        local(key_hbm, key_ref),
-        local(value_hbm, value_ref),
+        local(pair_hbm, pair_ref),
         local(time_hbm, time_ref),
         local(window_hbm, window_ref),
     ]
@@ -181,9 +178,10 @@
     sin_k = jnp.concatenate([jnp.sin(own_angles)] * (WIDTH // 128), axis=1)
     for copy in small:
         copy.wait()
-    raw_k = key_ref[...].astype(F32)
+    own_pair = pair_ref[...].astype(F32)
+    raw_k = own_pair[:SPAN]
     near_kv[0] = jnp.concatenate(
-        [raw_k * cos_k + turned(raw_k) * sin_k, value_ref[...].astype(F32)], axis=0
+        [raw_k * cos_k + turned(raw_k) * sin_k, own_pair[SPAN:]], axis=0
     ).astype(BF)
 
     pl.semaphore_wait(barrier, len(greet))
@@ -599,8 +597,7 @@
 
     inputs = (
         video_query[0],
-        audio_key[0],
-        audio_value[0],
+        jnp.concatenate([audio_key[0], audio_value[0]], axis=0),
         out_weight,
         grad_out[0],
         query_time.reshape(1, TOK),
@@ -614,11 +611,10 @@
         body,
         name="fused",
         out_shape=[pltpu.VMEM(shape, dtype) for shape, dtype in results],
-        in_specs=[hbm] * 7,
+        in_specs=[hbm] * 6,
         out_specs=[vmem] * 5,
         scratch_shapes=[
-            pltpu.VMEM((SPAN, WIDTH), BF),
-            pltpu.VMEM((SPAN, WIDTH), BF),
+            pltpu.VMEM((2 * SPAN, WIDTH), BF),
             pltpu.VMEM((1, TOK), jnp.int32),
             pltpu.VMEM((2, TOK), jnp.int32),
             pltpu.VMEM((GROUPS, TOK, GW), BF),

time: 60 us -> 61.1 us (1.018)
  other arithmetic: 0 us -> 1.35 us
    concatenate x0 -> x1, other arithmetic: none -> 1.35 us  [local(): jnp.concatenate([audio_key[0], audio_value[0]], axis=0)]
where the time goes in v6:
time: 61.1 us; the launch traced here: 60.9 us
  Pallas kernels  58.9 us (96%)
  other arithmetic  1.35 us (2%)
  between operations  0.64 us (1%)
    pallas_call x1, Pallas kernels, local(): pl.pallas_call(body, name='fused', out_shape=[pltpu.VMEM(shape, dtype) fo...  56.5 us
    pallas_call x1, Pallas kernels, local(): pl.pallas_call(finish, name='finish', out_shape=[jax.ShapeDtypeStruct(sha...  2.4 us
    concatenate x1, other arithmetic, local(): jnp.concatenate([audio_key[0], audio_value[0]], axis=0)  1.35 us

profile of v6, /device:TPU:4, one launch (start us, length us, event | category | flops | bytes accessed | tf_op | source)
XLA Modules:
  0.0 60.9 jit_solution(6903391143073497253)
XLA Ops:
  0.6 1.4 %pad_maximum_fusion.refs_1_ = bf16[16,1024]{1,0:T(8,128)(2,1)} fusion(bf16[8,1024]{1,0:T(8,128)(2,1)} %bitcast.11, bf16[8,1024]{1,0:T(8,128)(2,1)} %bitcast.12), kind=kLoop, calls=%fused_computation | loop fusion | flops 65536 | bytes 65536 | tf_op jit(solution)/shard_map/concatenate | solution.py:600
  2.0 56.5 %fused.1 = (bf16[512,4096]{1,0:T(8,128)(2,1)S(1)}, bf16[512,1024]{1,0:T(8,128)(2,1)S(1)}, f32[8,1024]{1,0:T(8,128)S(1)}, f32[8,1024]{1,0:T(8,128)S(1)}, f32[16,1024]{1,0:T(8,128)S(1)}) custom-call(bf16[512,1024]{1,0:T(8,128)(2,1)} %bitcast.10, bf16[16,1024]{1,0:T(8,128)(2,1)} %pad_maximum_fusion.refs_1_, bf16[1024,1024]{1,0:T(8,128)(2,1)} %refs_2_.1, ...), custom_call_target="tpu_custom_call" | custom-call | tf_op jit(solution)/shard_map/fused/pallas_call | solution.py:610
  58.4 2.4 %finish.1 = (bf16[512,4096]{1,0:T(8,128)(2,1)}, bf16[512,1024]{1,0:T(8,128)(2,1)}, f32[8,1024]{1,0:T(8,128)}, f32[8,1024]{1,0:T(8,128)}, f32[16,1024]{1,0:T(8,128)}) custom-call(bf16[512,4096]{1,0:T(8,128)(2,1)S(1)} %get-tuple-element.15.refs_0_, bf16[512,1024]{1,0:T(8,128)(2,1)S(1)} %get-tuple-element.16.refs_1_, f32[8,1024]{1,0:T(8,128)S(1)} %get-tuple-element.17.refs_2_, ...), custom_call_target="tpu_custom_call" | custom-call | tf_op jit(solution)/shard_map/finish/pallas_call | solution.py:661
